TPU v7x, 256 devices: a whole 4x4x8 slice. The times are simulated.
256 devices in a mesh: tm: 32 (over x, z_lo, core), tok: 8 (over y, z_hi).
Axes of the slice: x: 4, y: 4, z: 8 (z_hi: 2, z_lo: 4; z = z_hi * 4 + z_lo), core: 2. Of those that a mesh axis runs over, the one named last changes fastest.
Arguments:
- tokens: bfloat16 [32, 832, 512], P('tm', 'tok'), may hold values from -41 to 41
- attn_gain: float32 [512], replicated, may hold values from 0.1 to 1.9
- query_weight: bfloat16 [512, 512], replicated, may hold values from -2 to 2
- key_weight: bfloat16 [512, 512], replicated, may hold values from -2 to 2
- value_weight: bfloat16 [512, 512], replicated, may hold values from -0.25 to 0.25
- out_weight: bfloat16 [512, 512], replicated, may hold values from -0.25 to 0.25
- first_gain: float32 [512], replicated, may hold values from 0.1 to 1.9
- first_conv: bfloat16 [3, 3, 3, 512, 512], P(None, None, None, None, 'tok'), may hold values from -0.0546875 to 0.0546875
- second_gain: float32 [512], P('tok'), may hold values from 0.1 to 1.9
- second_conv: bfloat16 [3, 3, 3, 512, 512], P(None, None, None, 'tok'), may hold values from -0.0546875 to 0.0546875
Outputs:
- mixed: bfloat16 [32, 832, 512], P('tm', 'tok')
All inputs are finite; a program needn't handle non-finite values.
Results may differ from a plain program's by a relative error of at most 0.012.
Values may be sent and summed in bfloat16 or wider, within the bound.
A program may use at most 64 MiB of HBM per device.

v0:
```python
import math

import jax
import jax.numpy as jnp
from jax import lax
from jax.sharding import PartitionSpec as P

C = 512
GROUPS = 32
ROWS = 8
COLS = 104


EPSILON = 1e-06


def from_behind(block, axis, distance):
    devices = range(lax.axis_size(axis))
    route = [(i - distance, i) for i in devices if i - distance in devices]
    return lax.ppermute(block, axis, route)


def local_sums(values_in, group_width):
    dims_in = values_in.shape
    grouped = values_in.reshape(dims_in[:-1] + (dims_in[-1] // group_width, group_width))
    return (jnp.sum(grouped, axis=(-3, -1)), jnp.sum(grouped * grouped, axis=(-3, -1)))


def group_moments(totals, squares, entries):
    group_mean = totals / entries
    return (group_mean, squares / entries - group_mean * group_mean)


def normalize(values_in, group_mean, group_var, gain, group_width):
    dims_in = values_in.shape
    grouped = values_in.reshape(dims_in[:-1] + (dims_in[-1] // group_width, group_width))
    scaled = (grouped - group_mean[..., None, :, None]) * lax.rsqrt(group_var + EPSILON)[
        ..., None, :, None
    ]
    return scaled.reshape(dims_in) * gain


def edge_frames(current, one_back, two_back, frame_index):
    earlier = jnp.where(frame_index >= 1, one_back, current)
    earliest = jnp.where(frame_index >= 2, two_back, earlier)
    return jnp.stack([earliest, earlier, current])


def spatial_pad(frames):
    grid = frames.reshape(frames.shape[0], ROWS, COLS, frames.shape[2])
    return jnp.pad(grid, ((0, 0), (1, 1), (1, 1), (0, 0)), mode="edge")


def per_device(
    tokens,
    attn_gain,
    query_weight,
    key_weight,
    value_weight,
    out_weight,
    first_gain,
    first_conv,
    second_gain,
    second_conv,
):
    group_width = C // GROUPS
    score_scale = 1.0 / math.sqrt(C)
    frame_index = lax.axis_index("tm")
    own_rows = tokens[0].astype(jnp.float32)
    rows_dev = own_rows.shape[0]
    entries = rows_dev * lax.axis_size("tok") * group_width
    totals, squares = local_sums(own_rows, group_width)
    totals, squares = lax.psum((totals, squares), "tok")
    group_mean, group_var = group_moments(totals, squares, entries)
    normed = normalize(own_rows, group_mean, group_var, attn_gain, group_width).astype(jnp.bfloat16)
    queries = jnp.dot(normed, query_weight, preferred_element_type=jnp.float32).astype(jnp.bfloat16)
    key_rows = jnp.dot(normed, key_weight, preferred_element_type=jnp.float32).astype(jnp.bfloat16)
    value_rows = jnp.dot(normed, value_weight, preferred_element_type=jnp.float32).astype(
        jnp.bfloat16
    )
    attend_key_rows = lax.all_gather(key_rows, "tok", axis=0, tiled=True)
    attend_value_rows = lax.all_gather(value_rows, "tok", axis=0, tiled=True)
    running_max = jnp.full((rows_dev,), -jnp.inf, jnp.float32)
    running_sum = jnp.zeros((rows_dev,), jnp.float32)
    weighted = jnp.zeros((rows_dev, queries.shape[1]), jnp.float32)
    scores = (
        lax.dot_general(
            queries, attend_key_rows, (((1,), (1,)), ((), ())), preferred_element_type=jnp.float32
        )
        * score_scale
    )
    new_max = jnp.max(scores, axis=1)
    shrink = jnp.exp(running_max - new_max)
    exponent = jnp.exp(scores - new_max[:, None])
    running_sum = running_sum * shrink + jnp.sum(exponent, axis=1)
    weighted = weighted * shrink[:, None] + jnp.dot(
        exponent.astype(jnp.bfloat16), attend_value_rows, preferred_element_type=jnp.float32
    )
    running_max, running_sum, weighted = (new_max, running_sum, weighted)
    context = (weighted / running_sum[:, None]).astype(jnp.bfloat16)
    attended = (own_rows + jnp.dot(context, out_weight, preferred_element_type=jnp.float32)).astype(
        jnp.bfloat16
    )
    whole_frame = lax.all_gather(attended, "tok", axis=0, tiled=True)
    one_back = from_behind(whole_frame, "tm", 1)
    two_back = from_behind(whole_frame, "tm", 2)
    frames = edge_frames(whole_frame, one_back, two_back, frame_index)
    frame_vals = frames.astype(jnp.float32)
    totals, squares = local_sums(frame_vals, group_width)
    group_mean, group_var = group_moments(totals, squares, frame_vals.shape[1] * group_width)
    first_act = jax.nn.silu(
        normalize(frame_vals, group_mean, group_var, first_gain, group_width)
    ).astype(jnp.bfloat16)
    padded = spatial_pad(first_act)
    in_ch = first_act.shape[2]
    hidden = jnp.zeros((ROWS * COLS, first_conv.shape[4]), jnp.float32)
    for time_tap in range(3):
        for row_tap in range(3):
            for col_tap in range(3):
                window = padded[
                    time_tap, row_tap : row_tap + ROWS, col_tap : col_tap + COLS
                ].reshape(ROWS * COLS, in_ch)
                hidden = hidden + jnp.dot(
                    window,
                    first_conv[time_tap, row_tap, col_tap],
                    preferred_element_type=jnp.float32,
                )
    totals, squares = local_sums(hidden, group_width)
    group_mean, group_var = group_moments(totals, squares, ROWS * COLS * group_width)
    second_act = jax.nn.silu(
        normalize(hidden, group_mean, group_var, second_gain, group_width)
    ).astype(jnp.bfloat16)
    prior_act = from_behind(second_act, "tm", 1)
    earliest_act = from_behind(second_act, "tm", 2)
    padded_second = spatial_pad(edge_frames(second_act, prior_act, earliest_act, frame_index))
    local_ch = second_act.shape[1]
    columns = jnp.concatenate(
        [
            padded_second[time_tap, row_tap : row_tap + ROWS, col_tap : col_tap + COLS].reshape(
                ROWS * COLS, local_ch
            )
            for time_tap in range(3)
            for row_tap in range(3)
            for col_tap in range(3)
        ],
        axis=1,
    )
    flat_kernel = second_conv.reshape(27 * local_ch, second_conv.shape[4])
    conv_out = lax.psum_scatter(
        jnp.dot(columns, flat_kernel, preferred_element_type=jnp.float32).astype(jnp.bfloat16),
        "tok",
        scatter_dimension=0,
        tiled=True,
    ).astype(jnp.float32)
    result = (attended.astype(jnp.float32) + conv_out).astype(jnp.bfloat16)
    return result[None]


def solution(mesh):
    placed = (
        P("tm", "tok", None),
        P(),
        P(),
        P(),
        P(),
        P(),
        P(),
        P(None, None, None, None, "tok"),
        P("tok"),
        P(None, None, None, "tok", None),
    )
    return jax.shard_map(
        per_device, mesh=mesh, in_specs=placed, out_specs=P("tm", "tok", None), check_vma=False
    )
```

profile of v0, /device:TPU:2, one launch (start us, length us, event | category | flops | bytes accessed | tf_op | source)
XLA Modules:
  0.0 433.3 jit_solution(16661761613040685811)
XLA Ops:
  8.0 33.5 %all-reduce = (f32[32]{0:T(128)S(1)}, f32[32]{0:T(128)S(1)}) all-reduce(f32[32]{0:T(128)S(1)} %reduce_sum.96, f32[32]{0:T(128)S(1)} %reduce_sum.75), channel_id=1, replica_groups=mesh['tm'=32,'tok'=8] {'tok'}, use_global_device_ids=true, to_apply=%region_5.0 | all-reduce | flops 64 | bytes 512 | tf_op jit(solution)/shard_map/psum | solution.py:73
  41.8 1.4 convolution_convert_fusion.1
  43.2 50.4 %all_gather.10 = bf16[832,512]{1,0:T(8,128)(2,1)} all-gather(bf16[104,512]{1,0:T(8,128)(2,1)S(1)} %convolution_convert_fusion.1), channel_id=1, replica_groups=mesh['tm'=32,'tok'=8] {'tok'}, dimensions={0}, use_global_device_ids=true | all-gather | bytes 958464 | tf_op jit(solution)/shard_map/all_gather | solution.py:82
  93.6 1.3 convolution_convert_fusion.2
  94.9 50.0 %all_gather.9 = bf16[832,512]{1,0:T(8,128)(2,1)S(1)} all-gather(bf16[104,512]{1,0:T(8,128)(2,1)S(1)} %convolution_convert_fusion.2), channel_id=1, replica_groups=mesh['tm'=32,'tok'=8] {'tok'}, dimensions={0}, use_global_device_ids=true | all-gather | bytes 958464 | tf_op jit(solution)/shard_map/all_gather | solution.py:81
  145.0 1.7 fusion.98
  146.9 1.8 fusion.15
  149.4 51.1 %all_gather.11 = bf16[832,512]{1,0:T(8,128)(2,1)S(1)} all-gather(bf16[104,512]{1,0:T(8,128)(2,1)S(1)} %fusion.15), channel_id=1, replica_groups=mesh['tm'=32,'tok'=8] {'tok'}, dimensions={0}, use_global_device_ids=true | all-gather | bytes 958464 | tf_op jit(solution)/shard_map/all_gather | solution.py:104
  200.5 10.0 %collective-permute-start = (bf16[832,512]{1,0:T(8,128)(2,1)S(1)}, bf16[832,512]{1,0:T(8,128)(2,1)S(1)}, u32[]{:S(2)}, u32[]{:S(2)}) collective-permute-start(bf16[832,512]{1,0:T(8,128)(2,1)S(1)} %all_gather.11), channel_id=1, source_target_pairs={{0,16},{8,24},{16,32},{24,40},{32,48},{40,56},{48,64},{56,72},{64,... | collective-permute-start | bytes 2555912 | tf_op jit(solution)/shard_map/ppermute | solution.py:20
  210.5 2.1 collective-permute-start.1
  213.9 14.5 %collective-permute-done = bf16[832,512]{1,0:T(8,128)(2,1)S(1)} collective-permute-done((bf16[832,512]{1,0:T(8,128)(2,1)S(1)}, bf16[832,512]{1,0:T(8,128)(2,1)S(1)}, u32[]{:S(2)}, u32[]{:S(2)}) %collective-permute-start) | collective-permute-done | bytes 852000 | tf_op jit(solution)/shard_map/ppermute | solution.py:20
  229.3 2.5 broadcast_select_fusion.1
  231.7 2.2 copy.12
  235.2 2.6 convert_reduce_fusion
  238.3 2.6 multiply_convert_fusion
  241.0 1.8 fusion.8
  243.5 5.4 %fusion.91 = (bf16[1,8,104,512]{3,2,1,0:T(8,128)(2,1)S(1)}, bf16[1,8,104,512]{3,2,1,0:T(8,128)(2,1)S(1)}, bf16[1,8,104,512]{3,2,1,0:T(8,128)(2,1)S(1)}, bf16[1,8...) fusion(bf16[3,10,105,512]{3,2,1,0:T(8,128)(2,1)S(1)} %get-tuple, ...), kind=kLoop, calls=%fused_computation.190 | loop fusion | bytes 30670848 | tf_op jit(solution)/shard_map/slice | solution.py:120
  248.9 1.7 fusion.56
  251.9 1.6 convolution_add_fusion.24
  263.9 5.0 %collective-permute-start.2 = (bf16[832,64]{0,1:T(8,128)(2,1)S(1)}, bf16[832,64]{0,1:T(8,128)(2,1)S(1)}, u32[]{:S(2)}, u32[]{:S(2)}) collective-permute-start(bf16[832,64]{0,1:T(8,128)(2,1)S(1)} %multiply_convert_fusion.1), channel_id=1, source_target_pairs={{0,16},{8,24},{16,32},{24,40},{32,48},{40,56},{48,64},{56,72},{64,... | collective-permute-start | bytes 319496 | tf_op jit(solution)/shard_map/ppermute | solution.py:20
  268.9 2.1 collective-permute-start.3
  271.2 2.9 collective-permute-done.2
  274.1 3.5 collective-permute-done.3
  280.6 1.7 pad_maximum_fusion.12
  284.1 1.7 reshape_squeeze.184
  285.9 1.4 fusion.94
  287.2 1.8 reshape_squeeze.185
  290.1 1.6 constant_dynamic-update-slice_fusion.28
  291.7 1.6 constant_dynamic-update-slice_fusion.27
  295.7 1.7 reshape_squeeze.188
  297.4 1.7 reshape_squeeze.189
  299.1 1.7 reshape_squeeze.190
  300.8 1.7 reshape_squeeze.191
  302.5 1.7 reshape_squeeze.192
  304.3 1.7 reshape_squeeze.193
  307.7 1.6 constant_dynamic-update-slice_fusion.23
  309.3 1.6 constant_dynamic-update-slice_fusion.22
  310.9 1.5 constant_dynamic-update-slice_fusion.21
  312.4 1.6 constant_dynamic-update-slice_fusion.20
  314.0 1.5 constant_dynamic-update-slice_fusion.19
  315.5 1.6 constant_dynamic-update-slice_fusion.18
  320.0 1.7 reshape_squeeze.197
  323.4 1.6 constant_dynamic-update-slice_fusion.15
  324.9 1.6 constant_dynamic-update-slice_fusion.14
  326.5 1.6 constant_dynamic-update-slice_fusion.13
  335.3 4.5 %convolution_convert_fusion = bf16[832,512]{1,0:T(8,128)(2,1)} fusion(bf16[832,1728]{0,1:T(8,128)(2,1)} %constant_dynamic-update-slice_fusion.3, bf16[1728,512]{1,0:T(8,128)(2,1)S(1)} %bitcast.274), kind=kOutput, calls=%fused_computation.23 | convolution fusion | flops 1472626688 | bytes 5496832 | tf_op jit(solution)/shard_map/dot_general | solution.py:150
  339.9 85.0 %reduce-scatter.2.cloned.1.call-done = bf16[104,512]{1,0:T(8,128)(2,1)} async-done(((bf16[832,512]{1,0:T(8,128)(2,1)}), bf16[104,512]{1,0:T(8,128)(2,1)}) %reduce-scatter.2.cloned.1.call-update) | async-done | bytes 106512 | tf_op jit(solution)/shard_map/reduce_scatter | solution.py:149
  424.9 1.6 fusion.27
  (146 shorter events, 40.6 us)
Async XLA Ops:
  6.5 328.8 %copy-start = (bf16[3,3,3,64,512]{4,3,2,1,0:T(8,128)(2,1)S(1)}, bf16[3,3,3,64,512]{4,3,2,1,0:T(8,128)(2,1)}, u32[]{:S(2)}) copy-start(bf16[3,3,3,64,512]{4,3,2,1,0:T(8,128)(2,1)} %param.19) | copy-start | bytes 5308420
  6.5 138.4 %copy-start.9 = (bf16[1,104,512]{2,1,0:T(8,128)(2,1)S(1)}, bf16[1,104,512]{2,1,0:T(8,128)(2,1)}, u32[]{:S(2)}) copy-start(bf16[1,104,512]{2,1,0:T(8,128)(2,1)} %param.10) | copy-start | bytes 319492
  6.5 138.4 %copy-start.19 = (f32[512]{0:T(512)S(1)}, f32[512]{0:T(512)}, u32[]{:S(2)}) copy-start(f32[512]{0:T(512)} %param.11) | copy-start | bytes 6148
  6.5 418.3 %reduce-scatter.2.cloned.1.call-start = ((), (), s32[]{:S(2)}) async-start(), calls=%async_computation.1 | async-start | bytes 958464 | tf_op jit(solution)/shard_map/reduce_scatter | solution.py:149
  148.7 0.6 copy-start.17
  200.5 27.9 %collective-permute-start = (bf16[832,512]{1,0:T(8,128)(2,1)S(1)}, bf16[832,512]{1,0:T(8,128)(2,1)S(1)}, u32[]{:S(2)}, u32[]{:S(2)}) collective-permute-start(bf16[832,512]{1,0:T(8,128)(2,1)S(1)} %all_gather.11), channel_id=1, source_target_pairs={{0,16},{8,24},{16,32},{24,40},{32,48},{40,56},{48,64},{56,72},{64,... | collective-permute-start | bytes 2555912 | tf_op jit(solution)/shard_map/ppermute | solution.py:20
  210.5 18.8 %collective-permute-start.1 = (bf16[832,512]{1,0:T(8,128)(2,1)S(1)}, bf16[832,512]{1,0:T(8,128)(2,1)}, u32[]{:S(2)}, u32[]{:S(2)}) collective-permute-start(bf16[832,512]{1,0:T(8,128)(2,1)S(1)} %all_gather.11), channel_id=1, source_target_pairs={{0,8},{8,16},{16,24},{24,32},{32,40},{40,48},{48,56},{56,64},{64,7... | collective-permute-start | bytes 2555912 | tf_op jit(solution)/shard_map/ppermute | solution.py:20
  228.4 0.9 copy-start.10
  231.7 6.5 %copy-start.21 = (f32[512]{0:T(512)S(1)}, f32[512]{0:T(512)}, u32[]{:S(2)}) copy-start(f32[512]{0:T(512)} %param.16) | copy-start | bytes 6148
  248.9 4.6 %copy-start.7 = (bf16[1,8,104,512]{3,2,1,0:T(8,128)(2,1)S(1)}, bf16[1,8,104,512]{3,2,1,0:T(8,128)(2,1)}, u32[]{:S(2)}) copy-start(bf16[1,8,104,512]{3,2,1,0:T(8,128)(2,1)} %get-tuple-element.96) | copy-start | bytes 2555908
  248.9 4.6 %copy-start.8 = (bf16[3,3,3,512,64]{3,4,2,1,0:T(8,128)(2,1)S(1)}, bf16[3,3,3,512,64]{3,4,2,1,0:T(8,128)(2,1)}, u32[]{:S(2)}) copy-start(bf16[3,3,3,512,64]{3,4,2,1,0:T(8,128)(2,1)} %param.17) | copy-start | bytes 5308420
  248.9 5.4 %copy-start.6 = (bf16[1,8,104,512]{3,2,1,0:T(8,128)(2,1)S(1)}, bf16[1,8,104,512]{3,2,1,0:T(8,128)(2,1)}, u32[]{:S(2)}) copy-start(bf16[1,8,104,512]{3,2,1,0:T(8,128)(2,1)} %get-tuple-element.24) | copy-start | bytes 2555908
  251.9 2.8 copy-start.5
  253.9 1.6 copy-start.4
  254.3 1.6 copy-start.3
  255.1 1.6 copy-start.2
  255.5 1.6 copy-start.1
  261.3 2.4 copy-start.20
  263.9 10.2 %collective-permute-start.2 = (bf16[832,64]{0,1:T(8,128)(2,1)S(1)}, bf16[832,64]{0,1:T(8,128)(2,1)S(1)}, u32[]{:S(2)}, u32[]{:S(2)}) collective-permute-start(bf16[832,64]{0,1:T(8,128)(2,1)S(1)} %multiply_convert_fusion.1), channel_id=1, source_target_pairs={{0,16},{8,24},{16,32},{24,40},{32,48},{40,56},{48,64},{56,72},{64,... | collective-permute-start | bytes 319496 | tf_op jit(solution)/shard_map/ppermute | solution.py:20
  268.9 8.8 %collective-permute-start.3 = (bf16[832,64]{0,1:T(8,128)(2,1)S(1)}, bf16[832,64]{0,1:T(8,128)(2,1)S(1)}, u32[]{:S(2)}, u32[]{:S(2)}) collective-permute-start(bf16[832,64]{0,1:T(8,128)(2,1)S(1)} %multiply_convert_fusion.1), channel_id=1, source_target_pairs={{0,8},{8,16},{16,24},{24,32},{32,40},{40,48},{48,56},{56,64},{64,7... | collective-permute-start | bytes 319496 | tf_op jit(solution)/shard_map/ppermute | solution.py:20
  287.2 31.1 %copy-start.15 = (bf16[1,8,104,64]{2,1,3,0:T(8,128)(2,1)S(1)}, bf16[1,8,104,64]{2,1,3,0:T(8,128)(2,1)}, u32[]{:S(2)}) copy-start(bf16[1,8,104,64]{2,1,3,0:T(8,128)(2,1)} %get-tuple-element.55) | copy-start | bytes 319492
  287.2 31.9 %copy-start.12 = (bf16[1,8,104,64]{2,1,3,0:T(8,128)(2,1)S(1)}, bf16[1,8,104,64]{2,1,3,0:T(8,128)(2,1)}, u32[]{:S(2)}) copy-start(bf16[1,8,104,64]{2,1,3,0:T(8,128)(2,1)} %get-tuple-element.63) | copy-start | bytes 319492
  287.2 34.4 %copy-start.14 = (bf16[1,8,104,64]{2,1,3,0:T(8,128)(2,1)S(1)}, bf16[1,8,104,64]{2,1,3,0:T(8,128)(2,1)}, u32[]{:S(2)}) copy-start(bf16[1,8,104,64]{2,1,3,0:T(8,128)(2,1)} %get-tuple-element.54) | copy-start | bytes 319492
  289.0 32.8 %copy-start.11 = (bf16[1,8,104,64]{2,1,3,0:T(8,128)(2,1)S(1)}, bf16[1,8,104,64]{2,1,3,0:T(8,128)(2,1)}, u32[]{:S(2)}) copy-start(bf16[1,8,104,64]{2,1,3,0:T(8,128)(2,1)} %get-tuple-element.62) | copy-start | bytes 319492
  291.7 31.4 %copy-start.13 = (bf16[1,8,104,64]{2,1,3,0:T(8,128)(2,1)S(1)}, bf16[1,8,104,64]{2,1,3,0:T(8,128)(2,1)}, u32[]{:S(2)}) copy-start(bf16[1,8,104,64]{2,1,3,0:T(8,128)(2,1)} %get-tuple-element.53) | copy-start | bytes 319492
  309.3 23.1 %copy-start.16 = (bf16[1,8,104,64]{2,1,3,0:T(8,128)(2,1)S(1)}, bf16[1,8,104,64]{2,1,3,0:T(8,128)(2,1)}, u32[]{:S(2)}) copy-start(bf16[1,8,104,64]{2,1,3,0:T(8,128)(2,1)} %get-tuple-element.73) | copy-start | bytes 319492
  335.3 89.5 %copy-start.18 = (bf16[104,512]{1,0:T(8,128)(2,1)S(1)}, bf16[104,512]{1,0:T(8,128)(2,1)}, u32[]{:S(2)}) copy-start(bf16[104,512]{1,0:T(8,128)(2,1)} %copy-done.17) | copy-start | bytes 319492
Sparse Core Ops, SparseCore 0:
  340.0 84.7 reduce-scatter.1
where the time goes:
time: 434 us; the launch traced here: 433 us
  blocking collectives  185 us (43%)
  waiting for transfers between devices  106 us (24%)
  local copies, waits for them, and re-layouts  66.3 us (15%)
  matrix products  24.5 us (6%)
  starting transfers between devices  19.2 us (4%)
  other arithmetic  18.3 us (4%)
  between operations  14 us (3%)
    reduce_scatter x1, waiting for transfers between devices, per_device(): lax.psum_scatter(jnp.dot(columns, flat_kernel, preferred_element_type=jnp...  85 us
    all_gather x1, blocking collectives, per_device(): whole_frame = lax.all_gather(attended, 'tok', axis=0, tiled=True)  51.1 us
    all_gather x1, blocking collectives, per_device(): attend_value_rows = lax.all_gather(value_rows, 'tok', axis=0, tiled=True)  50.4 us
    all_gather x1, blocking collectives, per_device(): attend_key_rows = lax.all_gather(key_rows, 'tok', axis=0, tiled=True)  50 us
    psum x1, blocking collectives, per_device(): totals, squares = lax.psum((totals, squares), 'tok')  33.5 us
    unnamed x71, local copies, waits for them, and re-layouts  27.9 us
    another operation x24, local copies, waits for them, and re-layouts, per_device(): padded_second[time_tap, row_tap:row_tap + ROWS, col_tap:col_tap + COLS]  22.8 us
    ppermute x4, waiting for transfers between devices, from_behind(): return lax.ppermute(block, axis, route)  21 us
  transfers between devices with their start and end apart: 5, of which 4 were waited for; matrix products, arithmetic and copies ran while one was open for 0% of the time, Pallas kernels for 0%

commit v1 on v0

v1 whole, which is shorter than its diff:
```python
import math

import jax
import jax.numpy as jnp
from jax import lax
from jax.experimental import pallas as pl
from jax.experimental.pallas import tpu as pltpu
from jax.sharding import PartitionSpec as P

F32 = jnp.float32
BF16 = jnp.bfloat16
MESH = pl.DeviceIdType.MESH

C = 512
HALF = C // 2
ROWS = 8
COLS = 104
CELLS = ROWS * COLS
WIDTH = 16
LOCAL = 64
EPSILON = 1e-06

PAIRS = ((0, 0), (0, 2), (1, 0), (1, 2), (2, 0), (2, 2), (0, 1), (1, 1))
LAST = (2, 1)


def taps_of(time):
    return tuple((time,) + pair for pair in PAIRS)


FIRST_ORDER = (
    taps_of(0) + ((0,) + LAST, (1,) + LAST) + taps_of(1) + taps_of(2) + ((2,) + LAST,)
)
SECOND_ORDER = (
    taps_of(2) + taps_of(1) + taps_of(0) + ((1,) + LAST, (0,) + LAST, (2,) + LAST)
)
FIRST_PLACES = ((0, 512, 0), (640, 512, 1), (1152, 1664, 0))


def lane_low(shape):
    return lax.broadcasted_iota(jnp.int32, shape, len(shape) - 1) < 64


def row_before(x):
    return jnp.concatenate([x[0:1], x[0 : ROWS - 1]], axis=0)


def row_after(x):
    return jnp.concatenate([x[1:ROWS], x[ROWS - 1 : ROWS]], axis=0)


def col_before_after(x):
    col = lax.broadcasted_iota(jnp.int32, x.shape, 1)
    before = jnp.where(col == 0, x, pltpu.roll(x, 1, 1))
    after = jnp.where(col == COLS - 1, x, pltpu.roll(x, COLS - 1, 1))
    return jnp.where(lane_low(x.shape), before, after)


def group_matrix(period):
    i = lax.broadcasted_iota(jnp.int32, (128, 128), 0)
    k = lax.broadcasted_iota(jnp.int32, (128, 128), 1)
    same = ((i & (period - 1)) >> 4) == ((k & (period - 1)) >> 4)
    return jnp.where(same, 1.0, 0.0).astype(F32)


def moments(stacked, period, entries, n):
    totals = (
        jnp.dot(
            stacked,
            group_matrix(period),
            precision=lax.Precision.HIGHEST,
            preferred_element_type=F32,
        )
        / entries
    )
    mean = totals[0:n]
    var = totals[n : 2 * n] - mean * mean
    return mean, lax.rsqrt(var + EPSILON)


def wide_moments(total, square):
    pieces = [total[:, 128 * k : 128 * k + 128] for k in range(4)]
    pieces += [square[:, 128 * k : 128 * k + 128] for k in range(4)]
    mean, rstd = moments(jnp.concatenate(pieces, axis=0), 128, CELLS * WIDTH, 4)
    spread = lambda v: jnp.concatenate([v[k : k + 1] for k in range(4)], axis=1)
    return spread(mean), spread(rstd)


def silu(v):
    return v * (0.5 * jnp.tanh(0.5 * v) + 0.5)


def dot(a, b):
    return jnp.dot(a, b, preferred_element_type=F32)


def dot_t(a, b):
    return lax.dot_general(a, b, (((1,), (1,)), ((), ())), preferred_element_type=F32)


def kernel(
    tok, gain0, wq, wk, wv, wo, gain1, k1, gain2, k2, out,
    xg, x32, nb, wts, wm, wn, w1r, w1t, w2, gains, gain2v, act, zs, msg, acc, xown, xrest,
    ua, in1, in2, rs1s, rs1r, rs2s, rs2r, zsend, zrecv,
    load_sem, ag_send, ag_recv, fx_send, fx_recv, rs_send, rs_recv,
):
    me = lax.axis_index("tok")
    t = lax.axis_index("tm")
    frames = lax.axis_size("tm")
    y = me // 2
    h = me % 2
    o = 1 - h
    yp, ym, y2 = (y + 1) % 4, (y + 3) % 4, (y + 2) % 4
    up, down, across = 2 * yp + h, 2 * ym + h, 2 * y + o

    own = [
        pltpu.make_async_copy(
            tok.at[0, :, pl.ds(HALF * k, HALF)], xg.at[me, k], load_sem.at[k]
        )
        for k in range(2)
    ]
    for c in own:
        c.start()

    barrier = pltpu.get_barrier_semaphore()
    for there in (up, down, across):
        pl.semaphore_signal(barrier, inc=1, device_id={"tok": there}, device_id_type=MESH)

    @pl.when(t >= 1)
    def _():
        pl.semaphore_signal(barrier, inc=1, device_id={"tm": t - 1}, device_id_type=MESH)

    @pl.when(t >= 2)
    def _():
        pl.semaphore_signal(barrier, inc=1, device_id={"tm": t - 2}, device_id_type=MESH)

    small = [
        pltpu.make_async_copy(gain0, gains.at[0], load_sem.at[2]),
        pltpu.make_async_copy(gain1, gains.at[1], load_sem.at[3]),
        pltpu.make_async_copy(gain2, gain2v, load_sem.at[4]),
    ]
    mats = [
        pltpu.make_async_copy(w, wts.at[k], load_sem.at[5 + k])
        for k, w in enumerate((wq, wk, wv, wo))
    ]
    for c in mats + small:
        c.start()
    for k, (a, b, e) in enumerate(FIRST_ORDER):
        pltpu.make_async_copy(
            k1.at[a, b, e], w1r.at[pl.ds(LOCAL * k, LOCAL)], load_sem.at[9]
        ).start()
    for k, (a, b, e) in enumerate(SECOND_ORDER):
        pltpu.make_async_copy(
            k2.at[a, b, e], w2.at[pl.ds(LOCAL * k, LOCAL)], load_sem.at[10]
        ).start()

    def ag(block, half, there, k):
        return pltpu.make_async_remote_copy(
            src_ref=xg.at[block, half],
            dst_ref=xg.at[block, half],
            send_sem=ag_send.at[k],
            recv_sem=ag_recv.at[block, half],
            device_id={"tok": there},
            device_id_type=MESH,
        )

    gathered = []

    def ag_go(block, half, there):
        c = ag(block, half, there, len(gathered))
        c.start()
        gathered.append(c)

    def ag_wait(block, half):
        ag(block, half, across, 0).wait_recv()

    for c in own:
        c.wait()
    late = jnp.where(t < frames - 1, 1, 0) + jnp.where(t < frames - 2, 1, 0)
    pl.semaphore_wait(barrier, 3 + late)

    ag_go(me, 0, up)
    ag_go(me, 1, down)
    ag_go(me, 0, across)
    ag_go(me, 1, across)
    ag_go(me, 1, up)
    ag_go(me, 0, down)

    for c in mats[:2]:
        c.wait()
    wm[...] = (dot_t(wts[0], wts[1]) * (math.log2(math.e) / math.sqrt(C))).astype(BF16)

    ag_wait(2 * ym + h, 0)
    ag_go(2 * ym + h, 0, up)
    ag_wait(2 * yp + h, 1)
    ag_go(2 * yp + h, 1, down)

    for c in mats[2:]:
        c.wait()
    wn[...] = dot(wts[2], wts[3]).astype(BF16)

    ag_wait(across, 0)
    ag_go(across, 0, up)
    ag_go(across, 0, down)
    ag_wait(across, 1)
    ag_go(across, 1, down)
    ag_go(across, 1, up)

    pltpu.make_async_copy(w1r, w1r, load_sem.at[9]).wait()
    w1t[...] = w1r[...].T

    ag_wait(2 * ym + o, 0)
    ag_go(2 * ym + o, 0, up)
    ag_wait(2 * yp + o, 1)
    ag_go(2 * yp + o, 1, down)

    ag_wait(2 * ym + h, 1)
    ag_wait(2 * yp + h, 0)
    ag_wait(2 * y2 + h, 0)
    ag_wait(2 * y2 + h, 1)
    ag_wait(2 * ym + o, 1)
    ag_wait(2 * yp + o, 0)
    ag_wait(2 * y2 + o, 0)
    ag_wait(2 * y2 + o, 1)

    for c in small:
        c.wait()

    def collect(j, carry):
        total, square = carry
        rows = pl.ds(pl.multiple_of(j * COLS, 8), COLS)
        v = jnp.concatenate([xg[j, 0].astype(F32), xg[j, 1].astype(F32)], axis=1)
        x32[rows, :] = v
        return (
            total + jnp.sum(v, axis=0, keepdims=True),
            square + jnp.sum(v * v, axis=0, keepdims=True),
        )

    zero = jnp.zeros((1, C), F32)
    mean, rstd = wide_moments(*lax.fori_loop(0, ROWS, collect, (zero, zero)))
    scale = rstd * gains[0]

    def norm(k, carry):
        rows = pl.ds(pl.multiple_of(k * 208, 16), 208)
        nb[rows, :] = ((x32[rows, :] - mean) * scale).astype(BF16)
        return carry

    lax.fori_loop(0, 4, norm, 0)

    def attend(k, carry):
        total, square = carry
        rows = pl.ds(pl.multiple_of(k * 208, 16), 208)
        q = dot(nb[rows, :], wm[...]).astype(BF16)
        s = dot_t(q, nb[...])
        p = jnp.exp2(s - jnp.max(s, axis=1, keepdims=True))
        bottom = jnp.sum(p, axis=1, keepdims=True)
        context = (dot(p.astype(BF16), nb[...]) / bottom).astype(BF16)
        v = (x32[rows, :] + dot(context, wn[...])).astype(BF16).astype(F32)
        x32[rows, :] = v
        return (
            total + jnp.sum(v, axis=0, keepdims=True),
            square + jnp.sum(v * v, axis=0, keepdims=True),
        )

    mean, rstd = wide_moments(*lax.fori_loop(0, 4, attend, (zero, zero)))
    scale1 = rstd * gains[1]

    def activate(k, carry):
        rows = pl.ds(pl.multiple_of(k * 208, 16), 208)
        act[rows, :] = silu((x32[rows, :] - mean) * scale1).astype(BF16)
        return carry

    lax.fori_loop(0, 4, activate, 0)

    def fx(src, dst, there, k, slot):
        return pltpu.make_async_remote_copy(
            src_ref=src,
            dst_ref=dst,
            send_sem=fx_send.at[k],
            recv_sem=fx_recv.at[slot],
            device_id={"tm": there},
            device_id_type=MESH,
        )

    def columns(first, last):
        def one(k, carry):
            cols = pl.ds(pl.multiple_of(k * 256, 256), 256)
            zs[:, cols] = dot(act[...], w1t[:, cols])
            return carry

        lax.fori_loop(first, last, one, 0)
        if last == 6:
            zs[:, 1536:1728] = dot(act[...], w1t[:, 1536:1728])

    def fold(time):
        first, last, half = FIRST_PLACES[time]
        z = lambda c, n=128: zs[:, c : c + n].reshape(ROWS, COLS, n)
        low = lane_low((ROWS, COLS, 128))
        shifted = col_before_after(
            row_before(z(first)) + z(first + 128) + row_after(z(first + 256))
        )
        middle = z(first + 384)
        middle = jnp.where(low, row_before(middle), middle)
        if time < 2:
            extra = row_after(z(last))
        else:
            extra = jnp.concatenate(
                [row_after(z(last, 64)), jnp.zeros((ROWS, COLS, 64), F32)], axis=2
            )
        extra = jnp.where(low if half == 0 else ~low, extra, 0.0)
        total = shifted + middle + extra
        total = total + pltpu.roll(total, 64, 2)
        packed = jnp.where(low[0:4], total[0:4], total[4:8])
        return packed.reshape(CELLS // 2, 128)

    columns(0, 3)
    msg[0] = fold(0).astype(BF16)

    @pl.when(t < frames - 2)
    def _():
        fx(msg.at[0], in1.at[1], t + 2, 0, 1).start()

    @pl.when(t == 0)
    def _():
        fx(msg.at[0], in1.at[1], t + 1, 1, 1).start()
        in1[1] = msg[0]

    columns(3, 5)
    msg[1] = fold(1).astype(BF16)

    @pl.when(t < frames - 1)
    def _():
        fx(msg.at[1], in1.at[0], t + 1, 2, 0).start()

    @pl.when(t == 0)
    def _():
        in1[0] = msg[1]

    columns(5, 6)
    hidden = fold(2)

    @pl.when(t >= 1)
    def _():
        fx(msg.at[0], in1.at[1], t, 0, 1).wait_recv()
        fx(msg.at[1], in1.at[0], t, 2, 0).wait_recv()

    hidden = hidden + in1[0].astype(F32) + in1[1].astype(F32)

    pieces = [
        jnp.sum(hidden, axis=0, keepdims=True),
        jnp.sum(hidden * hidden, axis=0, keepdims=True),
        jnp.zeros((6, 128), F32),
    ]
    mean, rstd = moments(jnp.concatenate(pieces, axis=0), 64, CELLS * WIDTH, 1)
    gain = jnp.concatenate([gain2v[...], gain2v[...]], axis=1)
    u = silu((hidden - mean) * (rstd * gain)).astype(BF16)
    ua[...] = u

    @pl.when(t < frames - 1)
    def _():
        fx(ua, in2.at[0], t + 1, 3, 2).start()

    @pl.when(t < frames - 2)
    def _():
        fx(ua, in2.at[1], t + 2, 4, 3).start()

    @pl.when(t == 0)
    def _():
        fx(ua, in2.at[1], t + 1, 5, 3).start()
        in2[0] = ua[...]
        in2[1] = ua[...]

    def spread(dense):
        d = dense.astype(F32).reshape(4, COLS, 128)
        low = lane_low((4, COLS, 128))
        other = pltpu.roll(d, 64, 2)
        both = jnp.concatenate([jnp.where(low, d, other), jnp.where(low, other, d)], axis=0)
        sides = col_before_after(both)
        flat = lambda v: v.reshape(CELLS, 128)
        wide = [
            flat(row_before(sides)),
            flat(sides),
            flat(row_after(sides)),
            flat(jnp.where(lane_low(both.shape), row_before(both), both)),
        ]
        return wide, flat(row_after(both))

    pltpu.make_async_copy(w2, w2, load_sem.at[10]).wait()
    wide, last2 = spread(u)
    for k in range(4):
        xown[:, 128 * k : 128 * k + 128] = wide[k].astype(BF16)
    xrest[:, 1152:1216] = last2[:, 0:64].astype(BF16)

    def mine(k, carry):
        cols = pl.ds(pl.multiple_of(k * 256, 256), 256)
        acc[:, cols] = dot(xown[...], w2[0:512, cols])
        return carry

    lax.fori_loop(0, 2, mine, 0)

    @pl.when(t >= 1)
    def _():
        fx(ua, in2.at[0], t, 3, 2).wait_recv()

    wide, last1 = spread(in2[0])
    for k in range(4):
        xrest[:, 128 * k : 128 * k + 128] = wide[k].astype(BF16)

    @pl.when(t >= 1)
    def _():
        fx(ua, in2.at[1], t, 4, 3).wait_recv()

    wide, last0 = spread(in2[1])
    for k in range(4):
        xrest[:, 512 + 128 * k : 640 + 128 * k] = wide[k].astype(BF16)
    xrest[:, 1024:1152] = jnp.where(lane_low(last0.shape), last1, last0).astype(BF16)

    def partial_sums(where):
        rows = pl.ds(pl.multiple_of(where * 208, 16), 208)
        acc[rows, :] = acc[rows, :] + dot(xrest[rows, :], w2[512:1728, :])

    def piece(where, hh, half):
        rows = pl.ds(pl.multiple_of(where * 208 + hh * COLS, 8), COLS)
        return acc[rows, HALF * half : HALF * half + HALF]

    sent = []

    def rs_go(src, dst, there, recv):
        c = pltpu.make_async_remote_copy(
            src_ref=src,
            dst_ref=dst,
            send_sem=rs_send.at[len(sent)],
            recv_sem=rs_recv.at[recv],
            device_id={"tok": there},
            device_id_type=MESH,
        )
        c.start()
        sent.append(c)

    def rs_wait(dst, recv):
        pltpu.make_async_remote_copy(
            src_ref=dst,
            dst_ref=dst,
            send_sem=rs_send.at[0],
            recv_sem=rs_recv.at[recv],
            device_id={"tok": across},
            device_id_type=MESH,
        ).wait_recv()

    sides = (o, h)
    partial_sums(y2)
    for r in range(2):
        for half, there in ((0, up), (1, down)):
            rs1s[r, half] = piece(y2, sides[r], half).astype(BF16)
            rs_go(rs1s.at[r, half], rs1r.at[r, half], there, 2 * r + half)

    partial_sums(yp)
    for r in range(2):
        rs2s[r, 0, 1] = piece(yp, sides[r], 1).astype(BF16)
        rs_go(rs2s.at[r, 0, 1], rs2r.at[r, 0, 1], up, 4 + 4 * r + 1)
    partial_sums(ym)
    for r in range(2):
        rs2s[r, 1, 0] = piece(ym, sides[r], 0).astype(BF16)
        rs_go(rs2s.at[r, 1, 0], rs2r.at[r, 1, 0], down, 4 + 4 * r + 2)
    for r in range(2):
        rs_wait(rs1r.at[r, 0], 2 * r)
        rs2s[r, 0, 0] = (piece(yp, sides[r], 0) + rs1r[r, 0].astype(F32)).astype(BF16)
        rs_go(rs2s.at[r, 0, 0], rs2r.at[r, 0, 0], up, 4 + 4 * r)
        rs_wait(rs1r.at[r, 1], 2 * r + 1)
        rs2s[r, 1, 1] = (piece(ym, sides[r], 1) + rs1r[r, 1].astype(F32)).astype(BF16)
        rs_go(rs2s.at[r, 1, 1], rs2r.at[r, 1, 1], down, 4 + 4 * r + 3)
    partial_sums(y)

    def summed(r, half):
        for d in range(2):
            rs_wait(rs2r.at[r, d, half], 4 + 4 * r + 2 * d + half)
        return (
            piece(y, sides[r], half)
            + rs2r[r, 0, half].astype(F32)
            + rs2r[r, 1, half].astype(F32)
        )

    for half in (1, 0):
        zsend[half] = summed(0, half).astype(BF16)
        rs_go(zsend.at[half], zrecv.at[half], across, 12 + half)
    mine_rows = pl.ds(pl.multiple_of(me * COLS, 8), COLS)
    for half in (1, 0):
        cols = slice(HALF * half, HALF * half + HALF)
        v = summed(1, half) + x32[mine_rows, cols]
        rs_wait(zrecv.at[half], 12 + half)
        out[0, :, cols] = (v + zrecv[half].astype(F32)).astype(BF16)

    for c in gathered + sent:
        c.wait_send()

    @pl.when(t < frames - 2)
    def _():
        fx(msg.at[0], in1.at[1], t, 0, 1).wait_send()
        fx(ua, in2.at[1], t, 4, 3).wait_send()

    @pl.when(t < frames - 1)
    def _():
        fx(msg.at[1], in1.at[0], t, 2, 0).wait_send()
        fx(ua, in2.at[0], t, 3, 2).wait_send()

    @pl.when(t == 0)
    def _():
        fx(msg.at[0], in1.at[1], t, 1, 1).wait_send()
        fx(ua, in2.at[1], t, 5, 3).wait_send()


def per_device(tokens, gain0, wq, wk, wv, wo, gain1, k1, gain2, k2):
    dma = pltpu.SemaphoreType.DMA
    vmem = pltpu.VMEM
    return pl.pallas_call(
        kernel,
        out_shape=jax.ShapeDtypeStruct((1, COLS, C), BF16),
        in_specs=[pl.BlockSpec(memory_space=pl.ANY)] * 10,
        out_specs=pl.BlockSpec(memory_space=pltpu.VMEM),
        scratch_shapes=[
            vmem((ROWS, 2, COLS, HALF), BF16),
            vmem((CELLS, C), F32),
            vmem((CELLS, C), BF16),
            vmem((4, C, C), BF16),
            vmem((C, C), BF16),
            vmem((C, C), BF16),
            vmem((27 * LOCAL, C), BF16),
            vmem((C, 27 * LOCAL), BF16),
            vmem((27 * LOCAL, C), BF16),
            vmem((2, 1, C), F32),
            vmem((1, LOCAL), F32),
            vmem((CELLS, C), BF16),
            vmem((CELLS, 27 * LOCAL), F32),
            vmem((2, CELLS // 2, 128), BF16),
            vmem((CELLS, C), F32),
            vmem((CELLS, C), BF16),
            vmem((CELLS, 19 * LOCAL), BF16),
            vmem((CELLS // 2, 128), BF16),
            vmem((2, CELLS // 2, 128), BF16),
            vmem((2, CELLS // 2, 128), BF16),
            vmem((2, 2, COLS, HALF), BF16),
            vmem((2, 2, COLS, HALF), BF16),
            vmem((2, 2, 2, COLS, HALF), BF16),
            vmem((2, 2, 2, COLS, HALF), BF16),
            vmem((2, COLS, HALF), BF16),
            vmem((2, COLS, HALF), BF16),
            dma((11,)),
            dma((14,)),
            dma((ROWS, 2)),
            dma((6,)),
            dma((4,)),
            dma((14,)),
            dma((14,)),
        ],
        compiler_params=pltpu.CompilerParams(
            collective_id=0, has_side_effects=True, vmem_limit_bytes=56 * 2**20
        ),
    )(
        tokens,
        gain0.reshape(1, C),
        wq,
        wk,
        wv,
        wo,
        gain1.reshape(1, C),
        jnp.swapaxes(k1, 3, 4),
        gain2.reshape(1, LOCAL),
        k2,
    )


def solution(mesh):
    placed = (
        P("tm", "tok", None),
        P(),
        P(),
        P(),
        P(),
        P(),
        P(),
        P(None, None, None, None, "tok"),
        P("tok"),
        P(None, None, None, "tok", None),
    )
    return jax.shard_map(
        per_device, mesh=mesh, in_specs=placed, out_specs=P("tm", "tok", None), check_vma=False
    )
```

time: 434 us -> 58.8 us (0.14)
  blocking collectives: 185 us -> 0 us
  waiting for transfers between devices: 106 us -> 0 us
  local copies, waits for them, and re-layouts: 66.3 us -> 1.55 us
  Pallas kernels: 0 us -> 56.3 us
  matrix products: 24.5 us -> 0 us
  starting transfers between devices: 19.2 us -> 0 us
  other arithmetic: 18.3 us -> 0 us
  between operations: 14 us -> 0.01 us
    all_gather x3 -> x0, blocking collectives: 152 us -> none  [the longest x1 51.1 us: per_device(): whole_frame = lax.all_gather(attended, 'tok', axis=0, tiled=True)]
    reduce_scatter x1 -> x0, waiting for transfers between devices: 85 us -> none  [per_device(): lax.psum_scatter(jnp.dot(columns, flat_kernel, preferred_element_type=jnp...]
    pallas_call x0 -> x1, Pallas kernels: none -> 56.3 us  [per_device(): pl.pallas_call(kernel, out_shape=jax.ShapeDtypeStruct((1, COLS, C), BF16)...]
    psum x1 -> x0, blocking collectives: 33.5 us -> none  [per_device(): totals, squares = lax.psum((totals, squares), 'tok')]
    unnamed x71 -> x1, local copies, waits for them, and re-layouts: 27.9 us -> 1.55 us
    dot_general x32 -> x0, matrix products: 24.5 us -> none  [the longest x27 13.8 us: per_device(): jnp.dot(window, first_conv[time_tap, row_tap, col_tap], preferred_element...]
    another operation x28 -> x0, local copies, waits for them, and re-layouts: 23.3 us -> none  [the longest x24 22.8 us: per_device(): padded_second[time_tap, row_tap:row_tap + ROWS, col_tap:col_tap + COLS]]
    ppermute x4 -> x0, waiting for transfers between devices: 21 us -> none  [from_behind(): return lax.ppermute(block, axis, route)]
  transfers between devices with their start and end apart: 5 -> 0, of which waited for: 4 -> 0; matrix products, arithmetic and copies ran while one was open for 0% -> 0% of each run, Pallas kernels for 0% -> 0%
where the time goes in v1:
time: 58.8 us; the launch traced here: 57.8 us
  Pallas kernels  56.3 us (96%)
  local copies, waits for them, and re-layouts  1.55 us (3%)
    pallas_call x1, Pallas kernels, per_device(): pl.pallas_call(kernel, out_shape=jax.ShapeDtypeStruct((1, COLS, C), BF16)...  56.3 us
    unnamed x1, local copies, waits for them, and re-layouts  1.55 us

profile of v1, /device:TPU:2, one launch (start us, length us, event | category | flops | bytes accessed | tf_op | source)
XLA Modules:
  0.0 57.8 jit_solution(12401868009196365160)
XLA Ops:
  0.0 56.3 %shard_map.100 = bf16[1,104,512]{2,1,0:T(8,128)(2,1)} custom-call(bf16[1,104,512]{2,1,0:T(8,128)(2,1)} %tok.1, f32[1,512]{1,0:T(1,128)} %bitcast.5, bf16[512,512]{1,0:T(8,128)(2,1)} %wq.1, bf16[512,512]{1,0:T(8,128)(2,1)} %wk.1, bf16[512,512]{1,0:T(8,128)(2,1)} %wv.1, bf16[512,512]{1,0:T(8,128)(2,1)} %wo.1, f32[1,512]{1,0:T(1,128)} %bitcast.6, ...), custom_call_target="tpu_custom_call" | custom-call | tf_op jit(solution)/shard_map/pallas_call | solution.py:515
  56.3 1.5 %copy.12 = bf16[1,104,512]{2,1,0:T(8,128)(2,1)} copy(bf16[1,104,512]{2,1,0:T(8,128)(2,1)} %shard_map.100) | data formatting | bytes 212992

commit v2 on v1

v2 whole, which is shorter than its diff:
```python
import math

import jax
import jax.numpy as jnp
from jax import lax
from jax.experimental import pallas as pl
from jax.experimental.pallas import tpu as pltpu
from jax.sharding import PartitionSpec as P

F32 = jnp.float32
BF16 = jnp.bfloat16
MESH = pl.DeviceIdType.MESH

C = 512
HALF = C // 2
ROWS = 8
COLS = 104
CELLS = ROWS * COLS
WIDTH = 16
LOCAL = 64
EPSILON = 1e-06

ORDER = (0, 2, 4, 6, 1, 3, 5, 7)

PAIRS = ((0, 0), (0, 2), (1, 0), (1, 2), (2, 0), (2, 2), (0, 1), (1, 1))
LAST = (2, 1)


def taps_of(time):
    return tuple((time,) + pair for pair in PAIRS)


FIRST_ORDER = (
    taps_of(0) + ((0,) + LAST, (1,) + LAST) + taps_of(1) + taps_of(2) + ((2,) + LAST,)
)
SECOND_ORDER = (
    taps_of(2) + taps_of(1) + taps_of(0) + ((1,) + LAST, (0,) + LAST, (2,) + LAST)
)
FIRST_PLACES = ((0, 512, 0), (640, 512, 1), (1152, 1664, 0))


def lane_low(shape):
    return lax.broadcasted_iota(jnp.int32, shape, len(shape) - 1) < 64


def row_before(x):
    return jnp.concatenate([x[0:1], x[0 : ROWS - 1]], axis=0)


def row_after(x):
    return jnp.concatenate([x[1:ROWS], x[ROWS - 1 : ROWS]], axis=0)


def col_before_after(x):
    col = lax.broadcasted_iota(jnp.int32, x.shape, 1)
    before = jnp.where(col == 0, x, pltpu.roll(x, 1, 1))
    after = jnp.where(col == COLS - 1, x, pltpu.roll(x, COLS - 1, 1))
    return jnp.where(lane_low(x.shape), before, after)


def group_matrix(period):
    i = lax.broadcasted_iota(jnp.int32, (128, 128), 0)
    k = lax.broadcasted_iota(jnp.int32, (128, 128), 1)
    same = ((i & (period - 1)) >> 4) == ((k & (period - 1)) >> 4)
    return jnp.where(same, 1.0, 0.0).astype(F32)


def moments(stacked, period, entries, n):
    totals = (
        jnp.dot(
            stacked,
            group_matrix(period),
            precision=lax.Precision.HIGHEST,
            preferred_element_type=F32,
        )
        / entries
    )
    mean = totals[0:n]
    var = totals[n : 2 * n] - mean * mean
    return mean, lax.rsqrt(var + EPSILON)


def wide_moments(total, square):
    pieces = [total[:, 128 * k : 128 * k + 128] for k in range(4)]
    pieces += [square[:, 128 * k : 128 * k + 128] for k in range(4)]
    mean, rstd = moments(jnp.concatenate(pieces, axis=0), 128, CELLS * WIDTH, 4)
    spread = lambda v: jnp.concatenate([v[k : k + 1] for k in range(4)], axis=1)
    return spread(mean), spread(rstd)


def silu(v):
    return v * (0.5 * jnp.tanh(0.5 * v) + 0.5)


def dot(a, b):
    return jnp.dot(a, b, preferred_element_type=F32)


def dot_t(a, b):
    return lax.dot_general(a, b, (((1,), (1,)), ((), ())), preferred_element_type=F32)


def kernel(
    tok, gain0, wq, wk, wv, wo, gain1, k1, gain2, k2, out,
    stage, xg, x32, nb, wts, wm, wn, w1r, w1t, w2, gains, gain2v, act, zs, sums, hid, msg, acc,
    xown, xrest, ua, in1, in2, rss, rsr, zsend, zrecv, zdirect, near,
    load_sem, ag_send, ag_recv, fx_send, fx_recv, rs_send, rs_recv, z_send, z_recv, zd_send, zd_recv,
):
    me = lax.axis_index("tok")
    t = lax.axis_index("tm")
    frames = lax.axis_size("tm")
    y = me // 2
    h = me % 2
    o = 1 - h
    across = 2 * y + o

    def worker(frame):
        plane, place = frame // 8, frame % 8
        turned = 8 * plane + 2 * (3 - place // 2) + place % 2
        return jnp.where(plane % 2 == 1, turned, frame)

    f = worker(t)
    odd = (t // 8) % 2 == 1
    even = (t // 8) % 2 == 0
    middle = (t // 2) % 4
    outer = jnp.logical_and(odd, middle % 3 == 0)
    far = jnp.where(outer, h, o)
    close = 1 - far
    y2 = (y + 2) % 4
    beyond = 2 * y2 + far

    def beside(d):
        return 2 * ((y + d) % 4) + h

    dma = pltpu.make_async_copy

    own = [
        dma(tok.at[0, :, pl.ds(HALF * k, HALF)], stage.at[k], load_sem.at[k]) for k in range(2)
    ]
    kept = [
        dma(tok.at[0, :, pl.ds(HALF * k, HALF)], xg.at[me, k], load_sem.at[11 + k])
        for k in range(2)
    ]
    small = [
        dma(gain0, gains.at[0], load_sem.at[2]),
        dma(gain1, gains.at[1], load_sem.at[3]),
        dma(gain2, gain2v, load_sem.at[4]),
    ]
    mats = [dma(w, wts.at[k], load_sem.at[5 + k]) for k, w in enumerate((wq, wk, wv, wo))]
    barrier = pltpu.get_barrier_semaphore()

    def greet(**there):
        pl.semaphore_signal(barrier, inc=1, device_id=there, device_id_type=MESH)

    def load():
        for c in own:
            c.start()

        @pl.when(even)
        def _():
            for c in kept:
                c.start()

        @pl.when(even)
        def _():
            greet(tok=across)

        @pl.when(odd)
        def _():
            greet(tm=f, tok=across)
            greet(tm=f, tok=me)

        greet(tm=f, tok=beyond)
        for d in (2, 1, 3):
            greet(tok=beside(d))

        @pl.when(f >= 1)
        def _():
            greet(tm=worker(f - 1))

        @pl.when(f >= 2)
        def _():
            greet(tm=worker(f - 2))

    def all_entered():
        for c in own:
            c.wait()
        late = jnp.where(f < frames - 1, 1, 0) + jnp.where(f < frames - 2, 1, 0)
        pl.semaphore_wait(barrier, 5 + jnp.where(odd, 1, 0) + late)

    def load_weights():
        for c in mats + small:
            c.start()
        for k, (a, b, e) in enumerate(FIRST_ORDER):
            dma(k1.at[a, b, e], w1r.at[pl.ds(LOCAL * k, LOCAL)], load_sem.at[9]).start()
        for k, (a, b, e) in enumerate(SECOND_ORDER):
            dma(k2.at[a, b, e], w2.at[pl.ds(LOCAL * k, LOCAL)], load_sem.at[10]).start()

    def ag(src, block, half, k, **there):
        return pltpu.make_async_remote_copy(
            src_ref=src,
            dst_ref=xg.at[block, half],
            send_sem=ag_send.at[k],
            recv_sem=ag_recv.at[block, half],
            device_id=there,
            device_id_type=MESH,
        )

    def ag_wait(block, half):
        ag(stage.at[0], block, half, 0, tok=across).wait_recv()

    def own_send(half, k):
        there = (2 * y + far, beyond, 2 * y + close)[k]
        return ag(stage.at[half], 2 * y + h, half, 3 * half + k, tm=f, tok=there)

    def gather_own():
        for half in range(2):
            own_send(half, 0).start()

            @pl.when(odd)
            def _():
                own_send(half, 2).start()

        for half in range(2):
            own_send(half, 1).start()

    gathered = []

    def gather_side(side, first):
        block = 2 * y + side
        for half in range(2):
            if first:

                @pl.when(even)
                def _():
                    kept[half].wait()

                @pl.when(odd)
                def _():
                    ag_wait(block, half)

            else:
                ag_wait(block, half)
            for d in (2, 1, 3) if first else (1, 3):
                c = ag(xg.at[block, half], block, half, 6 + len(gathered), tok=beside(d))
                c.start()
                gathered.append(c)

    counted = [jnp.zeros((8, C), F32), jnp.zeros((8, C), F32)]

    def collect(block):
        v = jnp.concatenate([xg[block, 0].astype(F32), xg[block, 1].astype(F32)], axis=1)
        x32[pl.ds(pl.multiple_of(block * COLS, 8), COLS), :] = v
        v = v.reshape(COLS // 8, 8, C)
        counted[0] = counted[0] + jnp.sum(v, axis=0)
        counted[1] = counted[1] + jnp.sum(v * v, axis=0)

    def collect_side(side, ds, here):
        if here:
            collect(2 * y + side)
        for d in ds:
            block = 2 * ((y + d) % 4) + side
            for half in range(2):
                ag_wait(block, half)
            collect(block)

    def fold_scores():
        for c in mats[:2]:
            c.wait()
        wm[...] = (dot_t(wts[0], wts[1]) * (math.log2(math.e) / math.sqrt(C))).astype(BF16)

    def fold_values():
        for c in mats[2:]:
            c.wait()
        wn[...] = dot(wts[2], wts[3]).astype(BF16)

    def turn_first():
        dma(w1r, w1r, load_sem.at[9]).wait()
        w1t[...] = w1r[...].T

    def norm_tokens():
        for c in small:
            c.wait()

        total, square = (jnp.sum(v, axis=0, keepdims=True) for v in counted)
        mean, rstd = wide_moments(total, square)
        scale = rstd * gains[0]

        def norm(k, carry):
            rows = pl.ds(pl.multiple_of(k * 208, 16), 208)
            nb[rows, :] = ((x32[rows, :] - mean) * scale).astype(BF16)
            return carry

        lax.fori_loop(0, 4, norm, 0)

    def attention():
        q = dot(nb[...], wm[...]).astype(BF16)
        s = dot_t(q, nb[...])
        p = jnp.exp2(s - jnp.max(s, axis=1, keepdims=True))
        bottom = jnp.sum(p, axis=1, keepdims=True)
        context = (dot(p.astype(BF16), nb[...]) / bottom).astype(BF16)
        v = (x32[...] + dot(context, wn[...])).astype(BF16).astype(F32)
        x32[...] = v
        sums[0] = jnp.sum(v, axis=0, keepdims=True)
        sums[1] = jnp.sum(v * v, axis=0, keepdims=True)

    def activate():
        mean, rstd = wide_moments(sums[0], sums[1])
        scale = rstd * gains[1]

        def one(k, carry):
            rows = pl.ds(pl.multiple_of(k * 208, 16), 208)
            act[rows, :] = silu((x32[rows, :] - mean) * scale).astype(BF16)
            return carry

        lax.fori_loop(0, 4, one, 0)

    def fx(src, dst, there, k, slot):
        return pltpu.make_async_remote_copy(
            src_ref=src,
            dst_ref=dst,
            send_sem=fx_send.at[k],
            recv_sem=fx_recv.at[slot],
            device_id={"tm": there},
            device_id_type=MESH,
        )

    def columns(first, last):
        cols = slice(256 * first, min(256 * last, 27 * LOCAL))
        zs[:, cols] = dot(act[...], w1t[:, cols])

    def fold(time):
        first, last, half = FIRST_PLACES[time]
        z = lambda c, n=128: zs[:, c : c + n].reshape(ROWS, COLS, n)
        low = lane_low((ROWS, COLS, 128))
        shifted = col_before_after(
            row_before(z(first)) + z(first + 128) + row_after(z(first + 256))
        )
        middle = z(first + 384)
        middle = jnp.where(low, row_before(middle), middle)
        if time < 2:
            extra = row_after(z(last))
        else:
            extra = jnp.concatenate(
                [row_after(z(last, 64)), jnp.zeros((ROWS, COLS, 64), F32)], axis=2
            )
        extra = jnp.where(low if half == 0 else ~low, extra, 0.0)
        total = shifted + middle + extra
        total = total + pltpu.roll(total, 64, 2)
        packed = jnp.where(low[0:4], total[0:4], total[4:8])
        return packed.reshape(CELLS // 2, 128)

    def first_two_ahead():
        columns(0, 3)
        msg[0] = fold(0).astype(BF16)

    def send_two_ahead():
        @pl.when(f < frames - 2)
        def _():
            fx(msg.at[0], in1.at[1], worker(f + 2), 0, 1).start()

        @pl.when(f == 0)
        def _():
            fx(msg.at[0], in1.at[1], worker(f + 1), 1, 1).start()
            in1[1] = msg[0]

    def first_one_ahead():
        columns(3, 5)
        msg[1] = fold(1).astype(BF16)

    def send_one_ahead():
        @pl.when(f < frames - 1)
        def _():
            fx(msg.at[1], in1.at[0], worker(f + 1), 2, 0).start()

        @pl.when(f == 0)
        def _():
            in1[0] = msg[1]

    def first_own():
        columns(5, 7)
        hid[...] = fold(2)

    def wait_first():
        @pl.when(f >= 1)
        def _():
            fx(msg.at[0], in1.at[1], f, 0, 1).wait_recv()
            fx(msg.at[1], in1.at[0], f, 2, 0).wait_recv()

    def activate_second():
        hidden = hid[...] + in1[0].astype(F32) + in1[1].astype(F32)
        pieces = [
            jnp.sum(hidden, axis=0, keepdims=True),
            jnp.sum(hidden * hidden, axis=0, keepdims=True),
            jnp.zeros((6, 128), F32),
        ]
        mean, rstd = moments(jnp.concatenate(pieces, axis=0), 64, CELLS * WIDTH, 1)
        gain = jnp.concatenate([gain2v[...], gain2v[...]], axis=1)
        ua[...] = silu((hidden - mean) * (rstd * gain)).astype(BF16)

    def send_second():
        @pl.when(f < frames - 1)
        def _():
            fx(ua, in2.at[0], worker(f + 1), 3, 2).start()

        @pl.when(f < frames - 2)
        def _():
            fx(ua, in2.at[1], worker(f + 2), 4, 3).start()

        @pl.when(f == 0)
        def _():
            fx(ua, in2.at[1], worker(f + 1), 5, 3).start()
            in2[0] = ua[...]
            in2[1] = ua[...]

    def spread(dense):
        d = dense.astype(F32).reshape(4, COLS, 128)
        low = lane_low((4, COLS, 128))
        other = pltpu.roll(d, 64, 2)
        both = jnp.concatenate([jnp.where(low, d, other), jnp.where(low, other, d)], axis=0)
        sides = col_before_after(both)
        flat = lambda v: jnp.concatenate([v[r : r + 1] for r in ORDER], axis=0).reshape(CELLS, 128)
        wide = [
            flat(row_before(sides)),
            flat(sides),
            flat(row_after(sides)),
            flat(jnp.where(lane_low(both.shape), row_before(both), both)),
        ]
        return wide, flat(row_after(both))

    def second_own():
        dma(w2, w2, load_sem.at[10]).wait()
        wide, last = spread(ua[...])
        for k in range(4):
            xown[:, 128 * k : 128 * k + 128] = wide[k].astype(BF16)
        xrest[:, 1152:1216] = last[:, 0:64].astype(BF16)

        acc[...] = dot(xown[...], w2[0:512, :])

    def wait_second(back):
        @pl.when(f >= 1)
        def _():
            fx(ua, in2.at[back], f, 3 + back, 2 + back).wait_recv()

    def second_back():
        wide, last1 = spread(in2[0])
        for k in range(4):
            xrest[:, 128 * k : 128 * k + 128] = wide[k].astype(BF16)
        wait_second(1)
        wide, last0 = spread(in2[1])
        for k in range(4):
            xrest[:, 512 + 128 * k : 640 + 128 * k] = wide[k].astype(BF16)
        xrest[:, 1024:1152] = jnp.where(lane_low(last0.shape), last1, last0).astype(BF16)

    half_frame = CELLS // 2
    scattered = []

    def rs(r, half, d):
        return pltpu.make_async_remote_copy(
            src_ref=rss.at[r, half, (y + d) % 4],
            dst_ref=rsr.at[r, half, d - 1],
            send_sem=rs_send.at[r, half, d - 1],
            recv_sem=rs_recv.at[r, half, d - 1],
            device_id={"tok": beside(d)},
            device_id_type=MESH,
        )

    def sum_rows(r, side, half):
        rows = pl.ds(pl.multiple_of(side * half_frame, 16), half_frame)
        cols = slice(HALF * half, HALF * half + HALF)
        v = acc[rows, cols] + dot(xrest[rows, :], w2[512:1728, cols])
        acc[rows, cols] = v
        rss[r, half] = v.reshape(4, COLS, HALF).astype(BF16)

    def direct(half):
        return pltpu.make_async_remote_copy(
            src_ref=rss.at[0, half, y2],
            dst_ref=zdirect.at[half],
            send_sem=zd_send.at[half],
            recv_sem=zd_recv.at[half],
            device_id={"tm": f, "tok": beyond},
            device_id_type=MESH,
        )

    def send_rows(r, half):
        for d in (1, 3) if r == 0 else (2, 1, 3):
            c = rs(r, half, d)
            c.start()
            scattered.append(c)
        if r == 0:
            c = direct(half)
            c.start()
            scattered.append(c)

    def home(r, side, half):
        return pltpu.make_async_remote_copy(
            src_ref=zsend.at[r, half],
            dst_ref=zrecv.at[h, half],
            send_sem=z_send.at[r, half],
            recv_sem=z_recv.at[h, half],
            device_id={"tm": f, "tok": 2 * y + side},
            device_id_type=MESH,
        )

    def collect_rows(r, side, half):
        come = (1, 3) if r == 0 else (1, 3, 2)
        for d in come:
            rs(r, half, d).wait_recv()
        rows = pl.ds(pl.multiple_of(side * half_frame + y * COLS, 8), COLS)
        cols = slice(HALF * half, HALF * half + HALF)
        v = acc[rows, cols]
        for d in come:
            v = v + rsr[r, half, d - 1].astype(F32)
        own_rows = pl.ds(pl.multiple_of(me * COLS, 8), COLS)
        v = v + jnp.where(side == h, x32[own_rows, cols], 0.0)
        return v

    def scatter():
        for r, side in ((0, far), (1, close)):
            for half in range(2):
                sum_rows(r, side, half)
                send_rows(r, half)
        for half in range(2):
            zsend[0, half] = collect_rows(0, far, half).astype(BF16)
            home(0, far, half).start()
        for half in range(2):
            v = collect_rows(1, close, half)

            @pl.when(even)
            def _():
                near[half] = v

            @pl.when(odd)
            def _():
                zsend[1, half] = v.astype(BF16)
                home(1, close, half).start()

    def home_wait(source, half):
        pltpu.make_async_remote_copy(
            src_ref=zsend.at[0, half],
            dst_ref=zrecv.at[source, half],
            send_sem=z_send.at[0, half],
            recv_sem=z_recv.at[source, half],
            device_id={"tok": across},
            device_id_type=MESH,
        ).wait_recv()

    def last():
        for half in range(2):
            cols = slice(HALF * half, HALF * half + HALF)

            @pl.when(odd)
            def _():
                home_wait(h, half)
                near[half] = zrecv[h, half].astype(F32)

            direct(half).wait_recv()
            v = near[half] + zdirect[half].astype(F32)
            home_wait(o, half)
            out[0, :, cols] = (v + zrecv[o, half].astype(F32)).astype(BF16)

    def finish():
        for c in gathered + scattered:
            c.wait_send()
        for half in range(2):
            own_send(half, 0).wait_send()
            own_send(half, 1).wait_send()

            @pl.when(odd)
            def _():
                own_send(half, 2).wait_send()

    def finish_home():
        for half in range(2):
            home(0, far, half).wait_send()

            @pl.when(odd)
            def _():
                home(1, close, half).wait_send()

    def finish_frames():
        @pl.when(f < frames - 2)
        def _():
            fx(msg.at[0], in1.at[1], f, 0, 1).wait_send()
            fx(ua, in2.at[1], f, 4, 3).wait_send()

        @pl.when(f < frames - 1)
        def _():
            fx(msg.at[1], in1.at[0], f, 2, 0).wait_send()
            fx(ua, in2.at[0], f, 3, 2).wait_send()

        @pl.when(f == 0)
        def _():
            fx(msg.at[0], in1.at[1], f, 1, 1).wait_send()
            fx(ua, in2.at[1], f, 5, 3).wait_send()

    load()
    all_entered()
    gather_own()
    load_weights()
    gather_side(close, True)
    fold_scores()
    fold_values()
    collect_side(close, (1, 3), True)
    gather_side(far, False)
    turn_first()
    collect_side(close, (2,), False)
    collect_side(far, (1, 3, 2), True)
    norm_tokens()
    attention()
    activate()
    first_two_ahead()
    send_two_ahead()
    first_one_ahead()
    send_one_ahead()
    first_own()
    wait_first()
    activate_second()
    send_second()
    second_own()
    wait_second(0)
    second_back()
    scatter()
    last()
    finish()
    finish_home()
    finish_frames()


def per_device(tokens, gain0, wq, wk, wv, wo, gain1, k1, gain2, k2):
    dma = pltpu.SemaphoreType.DMA
    vmem = pltpu.VMEM
    return pl.pallas_call(
        kernel,
        out_shape=pltpu.VMEM((1, COLS, C), BF16),
        in_specs=[pl.BlockSpec(memory_space=pl.ANY)] * 10,
        out_specs=pl.BlockSpec(memory_space=pltpu.VMEM),
        scratch_shapes=[
            vmem((2, COLS, HALF), BF16),
            vmem((ROWS, 2, COLS, HALF), BF16),
            vmem((CELLS, C), F32),
            vmem((CELLS, C), BF16),
            vmem((4, C, C), BF16),
            vmem((C, C), BF16),
            vmem((C, C), BF16),
            vmem((27 * LOCAL, C), BF16),
            vmem((C, 27 * LOCAL), BF16),
            vmem((27 * LOCAL, C), BF16),
            vmem((2, 1, C), F32),
            vmem((1, LOCAL), F32),
            vmem((CELLS, C), BF16),
            vmem((CELLS, 27 * LOCAL), F32),
            vmem((2, 1, C), F32),
            vmem((CELLS // 2, 128), F32),
            vmem((2, CELLS // 2, 128), BF16),
            vmem((CELLS, C), F32),
            vmem((CELLS, C), BF16),
            vmem((CELLS, 19 * LOCAL), BF16),
            vmem((CELLS // 2, 128), BF16),
            vmem((2, CELLS // 2, 128), BF16),
            vmem((2, CELLS // 2, 128), BF16),
            vmem((2, 2, 4, COLS, HALF), BF16),
            vmem((2, 2, 3, COLS, HALF), BF16),
            vmem((2, 2, COLS, HALF), BF16),
            vmem((2, 2, COLS, HALF), BF16),
            vmem((2, COLS, HALF), BF16),
            vmem((2, COLS, HALF), F32),
            dma((13,)),
            dma((16,)),
            dma((ROWS, 2)),
            dma((6,)),
            dma((4,)),
            dma((2, 2, 3)),
            dma((2, 2, 3)),
            dma((2, 2)),
            dma((2, 2)),
            dma((2,)),
            dma((2,)),
        ],
        compiler_params=pltpu.CompilerParams(
            collective_id=0, has_side_effects=True, vmem_limit_bytes=56 * 2**20
        ),
    )(
        tokens,
        gain0.reshape(1, C),
        wq,
        wk,
        wv,
        wo,
        gain1.reshape(1, C),
        jnp.swapaxes(k1, 3, 4),
        gain2.reshape(1, LOCAL),
        k2,
    )


def solution(mesh):
    placed = (
        P("tm", "tok", None),
        P(),
        P(),
        P(),
        P(),
        P(),
        P(),
        P(None, None, None, None, "tok"),
        P("tok"),
        P(None, None, None, "tok", None),
    )
    return jax.shard_map(
        per_device, mesh=mesh, in_specs=placed, out_specs=P("tm", "tok", None), check_vma=False
    )
```

time: 58.8 us -> 55.7 us (0.947)
  the two profiles are of different devices: /device:TPU:2 before, /device:TPU:70 now
where the time goes in v2:
time: 55.7 us; the launch traced here: 55.5 us
  Pallas kernels  54.9 us (99%)
  local copies, waits for them, and re-layouts  0.65 us (1%)
    pallas_call x1, Pallas kernels, per_device(): pl.pallas_call(kernel, out_shape=pltpu.VMEM((1, COLS, C), BF16), in_specs...  54.9 us

profile of v2, /device:TPU:70, one launch (start us, length us, event | category | flops | bytes accessed | tf_op | source)
XLA Modules:
  0.0 55.5 jit_solution(15111421195675346785)
XLA Ops:
  0.0 54.9 %shard_map.100 = bf16[1,104,512]{2,1,0:T(8,128)(2,1)S(1)} custom-call(bf16[1,104,512]{2,1,0:T(8,128)(2,1)} %tok.1, f32[1,512]{1,0:T(1,128)} %bitcast.5, bf16[512,512]{1,0:T(8,128)(2,1)} %wq.1, bf16[512,512]{1,0:T(8,128)(2,1)} %wk.1, bf16[512,512]{1,0:T(8,128)(2,1)} %wv.1, bf16[512,512]{1,0:T(8,128)(2,1)} %wo.1, f32[1,512]{1,0:T(1,128)} %bitcast.6, ...), custom_call_target="tpu_custom_call" | custom-call | tf_op jit(solution)/shard_map/pallas_call | solution.py:633
  54.9 0.6 %copy.12 = bf16[1,104,512]{2,1,0:T(8,128)(2,1)} copy(bf16[1,104,512]{2,1,0:T(8,128)(2,1)S(1)} %shard_map.100) | data formatting | bytes 212992

commit v3 on v2

v3 whole, which is shorter than its diff:
```python
import math

import jax
import jax.numpy as jnp
from jax import lax
from jax.experimental import pallas as pl
from jax.experimental.pallas import tpu as pltpu
from jax.sharding import PartitionSpec as P

F32 = jnp.float32
BF16 = jnp.bfloat16
MESH = pl.DeviceIdType.MESH

C = 512
PIECES = 2
PIECE = C // PIECES
PARTS = 2
PART = C // PARTS
ROWS = 8
COLS = 104
CELLS = ROWS * COLS
WIDTH = 16
LOCAL = 64
EPSILON = 1e-06

ORDER = (0, 2, 4, 6, 1, 3, 5, 7)

PAIRS = ((0, 0), (0, 2), (1, 0), (1, 2), (2, 0), (2, 2), (0, 1), (1, 1))
LAST = (2, 1)


def taps_of(time):
    return tuple((time,) + pair for pair in PAIRS)


FIRST_ORDER = (
    taps_of(0) + ((0,) + LAST, (1,) + LAST) + taps_of(1) + taps_of(2) + ((2,) + LAST,)
)
SECOND_ORDER = (
    taps_of(2) + taps_of(0) + taps_of(1) + ((1,) + LAST, (0,) + LAST, (2,) + LAST)
)
FIRST_PLACES = ((0, 512, 0), (640, 512, 1), (1152, 1664, 0))


def lane_low(shape):
    return lax.broadcasted_iota(jnp.int32, shape, len(shape) - 1) < 64


def row_before(x):
    return jnp.concatenate([x[0:1], x[0 : ROWS - 1]], axis=0)


def row_after(x):
    return jnp.concatenate([x[1:ROWS], x[ROWS - 1 : ROWS]], axis=0)


def col_before_after(x):
    col = lax.broadcasted_iota(jnp.int32, x.shape, 1)
    before = jnp.where(col == 0, x, pltpu.roll(x, 1, 1))
    after = jnp.where(col == COLS - 1, x, pltpu.roll(x, COLS - 1, 1))
    return jnp.where(lane_low(x.shape), before, after)


def group_matrix(period):
    i = lax.broadcasted_iota(jnp.int32, (128, 128), 0)
    k = lax.broadcasted_iota(jnp.int32, (128, 128), 1)
    same = ((i & (period - 1)) >> 4) == ((k & (period - 1)) >> 4)
    return jnp.where(same, 1.0, 0.0).astype(F32)


def moments(stacked, period, entries, n):
    totals = (
        jnp.dot(
            stacked,
            group_matrix(period),
            precision=lax.Precision.HIGHEST,
            preferred_element_type=F32,
        )
        / entries
    )
    mean = totals[0:n]
    var = totals[n : 2 * n] - mean * mean
    return mean, lax.rsqrt(var + EPSILON)


def wide_moments(total, square):
    pieces = [total[:, 128 * k : 128 * k + 128] for k in range(4)]
    pieces += [square[:, 128 * k : 128 * k + 128] for k in range(4)]
    mean, rstd = moments(jnp.concatenate(pieces, axis=0), 128, CELLS * WIDTH, 4)
    spread = lambda v: jnp.concatenate([v[k : k + 1] for k in range(4)], axis=1)
    return spread(mean), spread(rstd)


def silu(v):
    return v * (0.5 * jnp.tanh(0.5 * v) + 0.5)


def dot(a, b):
    return jnp.dot(a, b, preferred_element_type=F32)


def dot_t(a, b):
    return lax.dot_general(a, b, (((1,), (1,)), ((), ())), preferred_element_type=F32)


def kernel(
    tok, gain0, wq, wk, wv, wo, gain1, k1, gain2, k2, out,
    xg, x32, nb, wts, wm, wn, w1r, w1t, w2, gains, gain2v, act, zs, sums, hid, msg, acc,
    xown, xrest, ua, in1, in2, rss, rsr, zsend, zrecv, zdirect, near,
    load_sem, ag_send, ag_recv, fx_send, fx_recv, rs_send, rs_recv, z_send, z_recv, zd_send, zd_recv,
):
    me = lax.axis_index("tok")
    f = lax.axis_index("tm")
    frames = lax.axis_size("tm")
    y = me // 2
    h = me % 2
    o = 1 - h
    across = 2 * y + o
    y2 = (y + 2) % 4
    beyond = 2 * y2 + o
    core = f % 2
    mate = f + 1 - 2 * core

    def beside(d):
        return 2 * ((y + d) % 4) + h

    dma = pltpu.make_async_copy

    own = [
        dma(tok.at[0, :, pl.ds(PIECE * k, PIECE)], xg.at[me, k], load_sem.at[11 + k])
        for k in range(PIECES)
    ]
    small = [
        dma(gain0, gains.at[0], load_sem.at[2]),
        dma(gain1, gains.at[1], load_sem.at[3]),
        dma(gain2, gain2v, load_sem.at[4]),
    ]
    mats = [dma(w, wts.at[k], load_sem.at[5 + k]) for k, w in enumerate((wq, wk, wv, wo))]
    barrier = pltpu.get_barrier_semaphore()

    def greet(**there):
        pl.semaphore_signal(barrier, inc=1, device_id=there, device_id_type=MESH)

    def load():
        for c in own:
            c.start()

        greet(tok=across)
        for d in (2, 1, 3):
            greet(tok=beside(d))

        greet(tm=mate)

        @pl.when(f >= 2)
        def _():
            greet(tm=f - 2)

        for c in mats + small:
            c.start()
        for k, (a, b, e) in enumerate(FIRST_ORDER):
            dma(k1.at[a, b, e], w1r.at[pl.ds(LOCAL * k, LOCAL)], load_sem.at[9]).start()
        for k, (a, b, e) in enumerate(SECOND_ORDER):
            dma(k2.at[a, b, e], w2.at[pl.ds(LOCAL * k, LOCAL)], load_sem.at[10]).start()

    def all_entered():
        for c in own:
            c.wait()
        pl.semaphore_wait(barrier, 5 + jnp.where(f < frames - 2, 1, 0))

    def ag(block, half, k, there):
        return pltpu.make_async_remote_copy(
            src_ref=xg.at[block, half],
            dst_ref=xg.at[block, half],
            send_sem=ag_send.at[k],
            recv_sem=ag_recv.at[block, half],
            device_id={"tok": there},
            device_id_type=MESH,
        )

    def ag_wait(block, half):
        ag(block, half, 0, across).wait_recv()

    gathered = []

    def ag_go(block, half, there):
        c = ag(block, half, len(gathered), there)
        c.start()
        gathered.append(c)

    def gather_own():
        for half in range(PIECES):
            ag_go(me, half, across)
            for d in (2, 1, 3):
                ag_go(me, half, beside(d))
            if half + 1 < PIECES:
                gathered[4 * half].wait_send()

    def gather_far():
        for half in range(PIECES):
            ag_wait(across, half)
            for d in (2, 1, 3):
                ag_go(across, half, beside(d))

    def fold_scores():
        for c in mats[:2]:
            c.wait()
        wm[...] = (dot_t(wts[0], wts[1]) * (math.log2(math.e) / math.sqrt(C))).astype(BF16)

    def fold_values():
        for c in mats[2:]:
            c.wait()
        wn[...] = dot(wts[2], wts[3]).astype(BF16)

    def turn_first():
        dma(w1r, w1r, load_sem.at[9]).wait()
        w1t[...] = w1r[...].T

    def gather_rest():
        for side in (h, o):
            for d in (1, 3, 2):
                for half in range(PIECES):
                    ag_wait(2 * ((y + d) % 4) + side, half)

    zero = jnp.zeros((1, C), F32)

    def norm_tokens():
        for c in small:
            c.wait()

        def collect(j, carry):
            total, square = carry
            rows = pl.ds(pl.multiple_of(j * COLS, 8), COLS)
            v = jnp.concatenate([xg[j, k].astype(F32) for k in range(PIECES)], axis=1)
            x32[rows, :] = v
            return (
                total + jnp.sum(v, axis=0, keepdims=True),
                square + jnp.sum(v * v, axis=0, keepdims=True),
            )

        mean, rstd = wide_moments(*lax.fori_loop(0, ROWS, collect, (zero, zero)))
        scale = rstd * gains[0]

        def norm(k, carry):
            rows = pl.ds(pl.multiple_of(k * 208, 16), 208)
            nb[rows, :] = ((x32[rows, :] - mean) * scale).astype(BF16)
            return carry

        lax.fori_loop(0, 4, norm, 0)

    def attention():
        q = dot(nb[...], wm[...]).astype(BF16)
        s = dot_t(q, nb[...])
        p = jnp.exp2(s - jnp.max(s, axis=1, keepdims=True))
        bottom = jnp.sum(p, axis=1, keepdims=True)
        context = (dot(p.astype(BF16), nb[...]) / bottom).astype(BF16)
        v = (x32[...] + dot(context, wn[...])).astype(BF16).astype(F32)
        x32[...] = v
        sums[0] = jnp.sum(v, axis=0, keepdims=True)
        sums[1] = jnp.sum(v * v, axis=0, keepdims=True)

    def activate():
        mean, rstd = wide_moments(sums[0], sums[1])
        scale = rstd * gains[1]

        def one(k, carry):
            rows = pl.ds(pl.multiple_of(k * 208, 16), 208)
            act[rows, :] = silu((x32[rows, :] - mean) * scale).astype(BF16)
            return carry

        lax.fori_loop(0, 4, one, 0)

    def fx(src, dst, there, k, slot):
        return pltpu.make_async_remote_copy(
            src_ref=src,
            dst_ref=dst,
            send_sem=fx_send.at[k],
            recv_sem=fx_recv.at[slot],
            device_id={"tm": there},
            device_id_type=MESH,
        )

    def columns(first, last):
        cols = slice(256 * first, min(256 * last, 27 * LOCAL))
        zs[:, cols] = dot(act[...], w1t[:, cols])

    def fold(time):
        first, last, half = FIRST_PLACES[time]
        z = lambda c, n=128: zs[:, c : c + n].reshape(ROWS, COLS, n)
        low = lane_low((ROWS, COLS, 128))
        shifted = col_before_after(
            row_before(z(first)) + z(first + 128) + row_after(z(first + 256))
        )
        middle = z(first + 384)
        middle = jnp.where(low, row_before(middle), middle)
        if time < 2:
            extra = row_after(z(last))
        else:
            extra = jnp.concatenate(
                [row_after(z(last, 64)), jnp.zeros((ROWS, COLS, 64), F32)], axis=2
            )
        extra = jnp.where(low if half == 0 else ~low, extra, 0.0)
        total = shifted + middle + extra
        total = total + pltpu.roll(total, 64, 2)
        packed = jnp.where(low[0:4], total[0:4], total[4:8])
        return packed.reshape(CELLS // 2, 128)

    def first_one_ahead():
        columns(3, 5)
        msg[0] = fold(1).astype(BF16)

    def one_ahead():
        return fx(msg.at[0], in1.at[0], mate, 0, 0)

    def first_two_ahead():
        columns(0, 3)
        msg[1] = fold(0).astype(BF16)

    def two_ahead():
        return fx(msg.at[1], in1.at[1], f + 2, 1, 1)

    def first_frame():
        return fx(msg.at[2], in1.at[1], mate, 2, 1)

    def send_two_ahead():
        @pl.when(f == 0)
        def _():
            msg[2] = msg[1]
            first_frame().start()

        @pl.when(core == 0)
        def _():
            one_ahead().wait_recv()
            msg[1] = (msg[1].astype(F32) + in1[0].astype(F32)).astype(BF16)

        @pl.when(f < frames - 2)
        def _():
            two_ahead().start()

    def send_one_ahead():
        one_ahead().start()

        @pl.when(f == 0)
        def _():
            in1[1] = (msg[0].astype(F32) + msg[2].astype(F32)).astype(BF16)

    def first_own():
        columns(5, 7)
        hid[...] = fold(2)

    def wait_first():
        @pl.when(core == 1)
        def _():
            one_ahead().wait_recv()

        @pl.when(f >= 1)
        def _():
            two_ahead().wait_recv()

    def activate_second():
        hidden = hid[...] + in1[1].astype(F32) + jnp.where(core == 1, in1[0].astype(F32), 0.0)
        pieces = [
            jnp.sum(hidden, axis=0, keepdims=True),
            jnp.sum(hidden * hidden, axis=0, keepdims=True),
            jnp.zeros((6, 128), F32),
        ]
        mean, rstd = moments(jnp.concatenate(pieces, axis=0), 64, CELLS * WIDTH, 1)
        gain = jnp.concatenate([gain2v[...], gain2v[...]], axis=1)
        ua[...] = silu((hidden - mean) * (rstd * gain)).astype(BF16)

    def near_second():
        return fx(ua, in2.at[0], mate, 3, 2)

    def far_second():
        return fx(ua, in2.at[1], f + 2, 4, 3)

    def passed_second():
        return fx(in2.at[1], in2.at[0], mate, 3, 2)

    def send_second():
        @pl.when(f < frames - 2)
        def _():
            far_second().start()

        @pl.when(core == 0)
        def _():
            near_second().start()

        @pl.when(f == 0)
        def _():
            in2[0] = ua[...]
            in2[1] = ua[...]

    def spread(dense):
        d = dense.astype(F32).reshape(4, COLS, 128)
        low = lane_low((4, COLS, 128))
        other = pltpu.roll(d, 64, 2)
        both = jnp.concatenate([jnp.where(low, d, other), jnp.where(low, other, d)], axis=0)
        sides = col_before_after(both)
        flat = lambda v: jnp.concatenate([v[r : r + 1] for r in ORDER], axis=0).reshape(CELLS, 128)
        wide = [
            flat(row_before(sides)),
            flat(sides),
            flat(row_after(sides)),
            flat(jnp.where(lane_low(both.shape), row_before(both), both)),
        ]
        return wide, flat(row_after(both))

    def second_own():
        dma(w2, w2, load_sem.at[10]).wait()
        wide, last = spread(ua[...])
        for k in range(4):
            xown[:, 128 * k : 128 * k + 128] = wide[k].astype(BF16)
        xrest[:, 1152:1216] = last[:, 0:64].astype(BF16)

        acc[...] = dot(xown[...], w2[0:512, :])

    passes = jnp.logical_and(core == 1, f >= 3)

    def wait_second():
        @pl.when(f >= 2)
        def _():
            far_second().wait_recv()

        @pl.when(passes)
        def _():
            passed_second().start()

        @pl.when(f == 1)
        def _():
            near_second().wait_recv()
            in2[1] = in2[0]

    def second_back():
        wide, last0 = spread(in2[1])
        for k in range(4):
            xrest[:, 128 * k : 128 * k + 128] = wide[k].astype(BF16)
        acc[...] = acc[...] + dot(xrest[:, 0:512], w2[512:1024, :])

        @pl.when(f >= 2)
        def _():
            near_second().wait_recv()

        wide, last1 = spread(in2[0])
        for k in range(4):
            xrest[:, 512 + 128 * k : 640 + 128 * k] = wide[k].astype(BF16)
        xrest[:, 1024:1152] = jnp.where(lane_low(last0.shape), last1, last0).astype(BF16)

    half_frame = CELLS // 2
    scattered = []

    def rs(r, half, d):
        return pltpu.make_async_remote_copy(
            src_ref=rss.at[r, half, (y + d) % 4],
            dst_ref=rsr.at[r, half, d - 1],
            send_sem=rs_send.at[r, half, d - 1],
            recv_sem=rs_recv.at[r, half, d - 1],
            device_id={"tok": beside(d)},
            device_id_type=MESH,
        )

    def sum_rows(r, side, half):
        rows = pl.ds(pl.multiple_of(side * half_frame, 16), half_frame)
        cols = slice(PART * half, PART * half + PART)
        v = acc[rows, cols] + dot(xrest[rows, 512:1216], w2[1024:1728, cols])
        acc[rows, cols] = v
        rss[r, half] = v.reshape(4, COLS, PART).astype(BF16)

    def direct(half):
        return pltpu.make_async_remote_copy(
            src_ref=rss.at[0, half, y2],
            dst_ref=zdirect.at[half],
            send_sem=zd_send.at[half],
            recv_sem=zd_recv.at[half],
            device_id={"tok": beyond},
            device_id_type=MESH,
        )

    def send_rows(r, half):
        for d in (1, 3) if r == 0 else (2, 1, 3):
            c = rs(r, half, d)
            c.start()
            scattered.append(c)
        if r == 0:
            direct(half).start()

    def home(half):
        return pltpu.make_async_remote_copy(
            src_ref=zsend.at[half],
            dst_ref=zrecv.at[half],
            send_sem=z_send.at[half],
            recv_sem=z_recv.at[half],
            device_id={"tok": across},
            device_id_type=MESH,
        )

    def collect_rows(r, side, half):
        come = (1, 3) if r == 0 else (1, 3, 2)
        for d in come:
            rs(r, half, d).wait_recv()
        rows = pl.ds(pl.multiple_of(side * half_frame + y * COLS, 8), COLS)
        cols = slice(PART * half, PART * half + PART)
        v = acc[rows, cols]
        for d in come:
            v = v + rsr[r, half, d - 1].astype(F32)
        return v

    def scatter():
        for half in range(PARTS):
            sum_rows(0, o, half)
            send_rows(0, half)
        for half in range(PARTS):
            sum_rows(1, h, half)
        for half in range(PARTS):
            send_rows(1, half)
        for half in range(PARTS):
            zsend[half] = collect_rows(0, o, half).astype(BF16)
            home(half).start()
        own_rows = pl.ds(pl.multiple_of(me * COLS, 8), COLS)
        for half in range(PARTS):
            cols = slice(PART * half, PART * half + PART)
            near[half] = collect_rows(1, h, half) + x32[own_rows, cols]

    def last():
        for half in range(PARTS):
            cols = slice(PART * half, PART * half + PART)
            direct(half).wait_recv()
            v = near[half] + zdirect[half].astype(F32)
            home(half).wait_recv()
            out[0, :, cols] = (v + zrecv[half].astype(F32)).astype(BF16)

    def finish():
        for k, c in enumerate(gathered + scattered):
            if k >= 4 * PIECES or k % 4 or k == 4 * (PIECES - 1):
                c.wait_send()

    def finish_home():
        for half in range(PARTS):
            home(half).wait_send()
            direct(half).wait_send()

    def finish_frames():
        one_ahead().wait_send()

        @pl.when(f < frames - 2)
        def _():
            two_ahead().wait_send()
            far_second().wait_send()

        @pl.when(f == 0)
        def _():
            first_frame().wait_send()

        @pl.when(core == 0)
        def _():
            near_second().wait_send()

        @pl.when(passes)
        def _():
            passed_second().wait_send()

    load()
    all_entered()
    gather_own()
    fold_scores()
    fold_values()
    gather_far()
    turn_first()
    gather_rest()
    norm_tokens()
    attention()
    activate()
    first_two_ahead()
    send_two_ahead()
    first_one_ahead()
    send_one_ahead()
    first_own()
    wait_first()
    activate_second()
    send_second()
    second_own()
    wait_second()
    second_back()
    scatter()
    last()
    finish()
    finish_home()
    finish_frames()


def per_device(tokens, gain0, wq, wk, wv, wo, gain1, k1, gain2, k2):
    dma = pltpu.SemaphoreType.DMA
    vmem = pltpu.VMEM
    return pl.pallas_call(
        kernel,
        out_shape=pltpu.VMEM((1, COLS, C), BF16),
        in_specs=[pl.BlockSpec(memory_space=pl.ANY)] * 10,
        out_specs=pl.BlockSpec(memory_space=pltpu.VMEM),
        scratch_shapes=[
            vmem((ROWS, PIECES, COLS, PIECE), BF16),
            vmem((CELLS, C), F32),
            vmem((CELLS, C), BF16),
            vmem((4, C, C), BF16),
            vmem((C, C), BF16),
            vmem((C, C), BF16),
            vmem((27 * LOCAL, C), BF16),
            vmem((C, 27 * LOCAL), BF16),
            vmem((27 * LOCAL, C), BF16),
            vmem((2, 1, C), F32),
            vmem((1, LOCAL), F32),
            vmem((CELLS, C), BF16),
            vmem((CELLS, 27 * LOCAL), F32),
            vmem((2, 1, C), F32),
            vmem((CELLS // 2, 128), F32),
            vmem((3, CELLS // 2, 128), BF16),
            vmem((CELLS, C), F32),
            vmem((CELLS, C), BF16),
            vmem((CELLS, 19 * LOCAL), BF16),
            vmem((CELLS // 2, 128), BF16),
            vmem((2, CELLS // 2, 128), BF16),
            vmem((2, CELLS // 2, 128), BF16),
            vmem((2, PARTS, 4, COLS, PART), BF16),
            vmem((2, PARTS, 3, COLS, PART), BF16),
            vmem((PARTS, COLS, PART), BF16),
            vmem((PARTS, COLS, PART), BF16),
            vmem((PARTS, COLS, PART), BF16),
            vmem((PARTS, COLS, PART), F32),
            dma((11 + PIECES,)),
            dma((7 * PIECES,)),
            dma((ROWS, PIECES)),
            dma((5,)),
            dma((4,)),
            dma((2, PARTS, 3)),
            dma((2, PARTS, 3)),
            dma((PARTS,)),
            dma((PARTS,)),
            dma((PARTS,)),
            dma((PARTS,)),
        ],
        compiler_params=pltpu.CompilerParams(
            collective_id=0, has_side_effects=True, vmem_limit_bytes=56 * 2**20
        ),
    )(
        tokens,
        gain0.reshape(1, C),
        wq,
        wk,
        wv,
        wo,
        gain1.reshape(1, C),
        jnp.swapaxes(k1, 3, 4),
        gain2.reshape(1, LOCAL),
        k2,
    )


def solution(mesh):
    placed = (
        P("tm", "tok", None),
        P(),
        P(),
        P(),
        P(),
        P(),
        P(),
        P(None, None, None, None, "tok"),
        P("tok"),
        P(None, None, None, "tok", None),
    )
    return jax.shard_map(
        per_device, mesh=mesh, in_specs=placed, out_specs=P("tm", "tok", None), check_vma=False
    )
```

time: 55.7 us -> 50.5 us (0.907)
  the two profiles are of different devices: /device:TPU:70 before, /device:TPU:2 now
where the time goes in v3:
time: 50.5 us; the launch traced here: 50.4 us
  Pallas kernels  49.8 us (99%)
  local copies, waits for them, and re-layouts  0.65 us (1%)
    pallas_call x1, Pallas kernels, per_device(): pl.pallas_call(kernel, out_shape=pltpu.VMEM((1, COLS, C), BF16), in_specs...  49.8 us

profile of v3, /device:TPU:2, one launch (start us, length us, event | category | flops | bytes accessed | tf_op | source)
XLA Modules:
  0.0 50.4 jit_solution(8859424641907147245)
XLA Ops:
  0.0 49.8 %shard_map.100 = bf16[1,104,512]{2,1,0:T(8,128)(2,1)S(1)} custom-call(bf16[1,104,512]{2,1,0:T(8,128)(2,1)} %tok.1, f32[1,512]{1,0:T(1,128)} %bitcast.5, bf16[512,512]{1,0:T(8,128)(2,1)} %wq.1, bf16[512,512]{1,0:T(8,128)(2,1)} %wk.1, bf16[512,512]{1,0:T(8,128)(2,1)} %wv.1, bf16[512,512]{1,0:T(8,128)(2,1)} %wo.1, f32[1,512]{1,0:T(1,128)} %bitcast.6, ...), custom_call_target="tpu_custom_call" | custom-call | tf_op jit(solution)/shard_map/pallas_call | solution.py:593
  49.8 0.6 %copy.12 = bf16[1,104,512]{2,1,0:T(8,128)(2,1)} copy(bf16[1,104,512]{2,1,0:T(8,128)(2,1)S(1)} %shard_map.100) | data formatting | bytes 212992

commit v4 on v3

--- a/solution.py
+++ b/solution.py
@@ -65,19 +65,16 @@
     i = lax.broadcasted_iota(jnp.int32, (128, 128), 0)
     k = lax.broadcasted_iota(jnp.int32, (128, 128), 1)
     same = ((i & (period - 1)) >> 4) == ((k & (period - 1)) >> 4)
-    return jnp.where(same, 1.0, 0.0).astype(F32)
+    return jnp.where(same, 1.0, 0.0).astype(BF16)
 
 
 def moments(stacked, period, entries, n):
-    totals = (
-        jnp.dot(
-            stacked,
-            group_matrix(period),
-            precision=lax.Precision.HIGHEST,
-            preferred_element_type=F32,
-        )
-        / entries
-    )
+    high = stacked.astype(BF16).astype(F32)
+    rest = stacked - high
+    middle = rest.astype(BF16).astype(F32)
+    terms = jnp.concatenate([high, middle, rest - middle], axis=0).astype(BF16)
+    grouped = dot(terms, group_matrix(period))
+    totals = (grouped[0:8] + grouped[8:16] + grouped[16:24]) / entries
     mean = totals[0:n]
     var = totals[n : 2 * n] - mean * mean
     return mean, lax.rsqrt(var + EPSILON)
@@ -91,8 +88,8 @@
     return spread(mean), spread(rstd)
 
 
-def silu(v):
-    return v * (0.5 * jnp.tanh(0.5 * v) + 0.5)
+def silu_of_twice(w):
+    return w * jnp.tanh(w) + w
 
 
 def dot(a, b):
@@ -105,9 +102,9 @@
 
 def kernel(
     tok, gain0, wq, wk, wv, wo, gain1, k1, gain2, k2, out,
-    xg, x32, nb, wts, wm, wn, w1r, w1t, w2, gains, gain2v, act, zs, sums, hid, msg, acc,
-    xown, xrest, ua, in1, in2, rss, rsr, zsend, zrecv, zdirect, near,
-    load_sem, ag_send, ag_recv, fx_send, fx_recv, rs_send, rs_recv, z_send, z_recv, zd_send, zd_recv,
+    xg, x32, nb, wts, wm, wn, w1r, w1t, w2, gains, gain2v, act, zs, sums, part, hid, msg, acc,
+    xown, xrest, ua, in1, in2, rss, rsr, zsend, zrecv, near,
+    in_sem, load_sem, ag_send, ag_recv, fx_send, fx_recv, rs_send, rs_recv, z_send, z_recv,
 ):
     me = lax.axis_index("tok")
     f = lax.axis_index("tm")
@@ -116,10 +113,10 @@
     h = me % 2
     o = 1 - h
     across = 2 * y + o
-    y2 = (y + 2) % 4
-    beyond = 2 * y2 + o
     core = f % 2
     mate = f + 1 - 2 * core
+    leaves = jnp.logical_and(f % 8 >= 6, f < frames - 2)
+    enters = jnp.logical_and(f % 8 < 2, f >= 8)
 
     def beside(d):
         return 2 * ((y + d) % 4) + h
@@ -153,7 +150,11 @@
 
         @pl.when(f >= 2)
         def _():
-            greet(tm=f - 2)
+            greet(tm=f - 2, tok=jnp.where(enters, across, me))
+
+        @pl.when(leaves)
+        def _():
+            greet(tm=f + 2, tok=across)
 
         for c in mats + small:
             c.start()
@@ -165,7 +166,15 @@
     def all_entered():
         for c in own:
             c.wait()
-        pl.semaphore_wait(barrier, 5 + jnp.where(f < frames - 2, 1, 0))
+        nexts = jnp.where(f < frames - 2, 1, 0) + jnp.where(enters, 1, 0)
+        pl.semaphore_wait(barrier, 5 + nexts)
+
+        @pl.when(enters)
+        def _():
+            pl.semaphore_signal(
+                in_sem, inc=1, device_id={"tm": f - 2, "tok": across}, device_id_type=MESH
+            )
+
 
     def ag(block, half, k, there):
         return pltpu.make_async_remote_copy(
@@ -215,29 +224,33 @@
         dma(w1r, w1r, load_sem.at[9]).wait()
         w1t[...] = w1r[...].T
 
-    def gather_rest():
-        for side in (h, o):
-            for d in (1, 3, 2):
-                for half in range(PIECES):
-                    ag_wait(2 * ((y + d) % 4) + side, half)
-
-    zero = jnp.zeros((1, C), F32)
+    def collect(block):
+        v = jnp.concatenate([xg[block, k].astype(F32) for k in range(PIECES)], axis=1)
+        x32[pl.ds(pl.multiple_of(block * COLS, 8), COLS), :] = v
+        v = v.reshape(COLS // 8, 8, C)
+        part[0] = part[0] + jnp.sum(v, axis=0)
+        part[1] = part[1] + jnp.sum(v * v, axis=0)
+
+    def collect_here():
+        part[...] = jnp.zeros((2, 8, C), F32)
+        collect(me)
+
+    def collect_side(side):
+        def one(d, carry):
+            block = 2 * ((y + d) % 4) + side
+            for half in range(PIECES):
+                ag_wait(block, half)
+            collect(block)
+            return carry
+
+        lax.fori_loop(1, 4, one, 0)
 
     def norm_tokens():
         for c in small:
             c.wait()
 
-        def collect(j, carry):
-            total, square = carry
-            rows = pl.ds(pl.multiple_of(j * COLS, 8), COLS)
-            v = jnp.concatenate([xg[j, k].astype(F32) for k in range(PIECES)], axis=1)
-            x32[rows, :] = v
-            return (
-                total + jnp.sum(v, axis=0, keepdims=True),
-                square + jnp.sum(v * v, axis=0, keepdims=True),
-            )
-
-        mean, rstd = wide_moments(*lax.fori_loop(0, ROWS, collect, (zero, zero)))
+        total, square = (jnp.sum(part[k], axis=0, keepdims=True) for k in range(2))
+        mean, rstd = wide_moments(total, square)
         scale = rstd * gains[0]
 
         def norm(k, carry):
@@ -260,11 +273,11 @@
 
     def activate():
         mean, rstd = wide_moments(sums[0], sums[1])
-        scale = rstd * gains[1]
+        scale = rstd * gains[1] * 0.5
 
         def one(k, carry):
             rows = pl.ds(pl.multiple_of(k * 208, 16), 208)
-            act[rows, :] = silu((x32[rows, :] - mean) * scale).astype(BF16)
+            act[rows, :] = silu_of_twice((x32[rows, :] - mean) * scale).astype(BF16)
             return carry
 
         lax.fori_loop(0, 4, one, 0)
@@ -332,6 +345,10 @@
             one_ahead().wait_recv()
             msg[1] = (msg[1].astype(F32) + in1[0].astype(F32)).astype(BF16)
 
+        @pl.when(leaves)
+        def _():
+            pl.semaphore_wait(in_sem, 1)
+
         @pl.when(f < frames - 2)
         def _():
             two_ahead().start()
@@ -365,7 +382,7 @@
         ]
         mean, rstd = moments(jnp.concatenate(pieces, axis=0), 64, CELLS * WIDTH, 1)
         gain = jnp.concatenate([gain2v[...], gain2v[...]], axis=1)
-        ua[...] = silu((hidden - mean) * (rstd * gain)).astype(BF16)
+        ua[...] = silu_of_twice((hidden - mean) * (rstd * gain * 0.5)).astype(BF16)
 
     def near_second():
         return fx(ua, in2.at[0], mate, 3, 2)
@@ -465,23 +482,11 @@
         acc[rows, cols] = v
         rss[r, half] = v.reshape(4, COLS, PART).astype(BF16)
 
-    def direct(half):
-        return pltpu.make_async_remote_copy(
-            src_ref=rss.at[0, half, y2],
-            dst_ref=zdirect.at[half],
-            send_sem=zd_send.at[half],
-            recv_sem=zd_recv.at[half],
-            device_id={"tok": beyond},
-            device_id_type=MESH,
-        )
-
     def send_rows(r, half):
-        for d in (1, 3) if r == 0 else (2, 1, 3):
+        for d in (2, 1, 3):
             c = rs(r, half, d)
             c.start()
             scattered.append(c)
-        if r == 0:
-            direct(half).start()
 
     def home(half):
         return pltpu.make_async_remote_copy(
@@ -494,13 +499,12 @@
         )
 
     def collect_rows(r, side, half):
-        come = (1, 3) if r == 0 else (1, 3, 2)
-        for d in come:
+        for d in (1, 3, 2):
             rs(r, half, d).wait_recv()
         rows = pl.ds(pl.multiple_of(side * half_frame + y * COLS, 8), COLS)
         cols = slice(PART * half, PART * half + PART)
         v = acc[rows, cols]
-        for d in come:
+        for d in (1, 2, 3):
             v = v + rsr[r, half, d - 1].astype(F32)
         return v
 
@@ -523,10 +527,8 @@
     def last():
         for half in range(PARTS):
             cols = slice(PART * half, PART * half + PART)
-            direct(half).wait_recv()
-            v = near[half] + zdirect[half].astype(F32)
             home(half).wait_recv()
-            out[0, :, cols] = (v + zrecv[half].astype(F32)).astype(BF16)
+            out[0, :, cols] = (near[half] + zrecv[half].astype(F32)).astype(BF16)
 
     def finish():
         for k, c in enumerate(gathered + scattered):
@@ -536,7 +538,6 @@
     def finish_home():
         for half in range(PARTS):
             home(half).wait_send()
-            direct(half).wait_send()
 
     def finish_frames():
         one_ahead().wait_send()
@@ -561,11 +562,14 @@
     load()
     all_entered()
     gather_own()
+    collect_here()
     fold_scores()
     fold_values()
     gather_far()
     turn_first()
-    gather_rest()
+    collect_side(h)
+    collect(across)
+    collect_side(o)
     norm_tokens()
     attention()
     activate()
@@ -581,10 +585,10 @@
     wait_second()
     second_back()
     scatter()
+    finish()
+    finish_frames()
     last()
-    finish()
     finish_home()
-    finish_frames()
 
 
 def per_device(tokens, gain0, wq, wk, wv, wo, gain1, k1, gain2, k2):
@@ -610,6 +614,7 @@
             vmem((CELLS, C), BF16),
             vmem((CELLS, 27 * LOCAL), F32),
             vmem((2, 1, C), F32),
+            vmem((2, 8, C), F32),
             vmem((CELLS // 2, 128), F32),
             vmem((3, CELLS // 2, 128), BF16),
             vmem((CELLS, C), F32),
@@ -622,8 +627,8 @@
             vmem((2, PARTS, 3, COLS, PART), BF16),
             vmem((PARTS, COLS, PART), BF16),
             vmem((PARTS, COLS, PART), BF16),
-            vmem((PARTS, COLS, PART), BF16),
             vmem((PARTS, COLS, PART), F32),
+            pltpu.SemaphoreType.REGULAR,
             dma((11 + PIECES,)),
             dma((7 * PIECES,)),
             dma((ROWS, PIECES)),
@@ -631,8 +636,6 @@
             dma((4,)),
             dma((2, PARTS, 3)),
             dma((2, PARTS, 3)),
-            dma((PARTS,)),
-            dma((PARTS,)),
             dma((PARTS,)),
             dma((PARTS,)),
         ],

time: 50.5 us -> 49.8 us (0.986)
  Pallas kernels: 49.8 us -> 48.9 us
    pallas_call x1, Pallas kernels: 49.8 us -> 48.9 us  [per_device(): pl.pallas_call(kernel, out_shape=pltpu.VMEM((1, COLS, C), BF16), in_specs...]
where the time goes in v4:
time: 49.8 us; the launch traced here: 49.5 us
  Pallas kernels  48.9 us (98%)
  local copies, waits for them, and re-layouts  0.65 us (1%)
    pallas_call x1, Pallas kernels, per_device(): pl.pallas_call(kernel, out_shape=pltpu.VMEM((1, COLS, C), BF16), in_specs...  48.9 us

profile of v4, /device:TPU:2, one launch (start us, length us, event | category | flops | bytes accessed | tf_op | source)
XLA Modules:
  0.0 49.5 jit_solution(2141524216967876205)
XLA Ops:
  0.0 48.9 %shard_map.100 = bf16[1,104,512]{2,1,0:T(8,128)(2,1)S(1)} custom-call(bf16[1,104,512]{2,1,0:T(8,128)(2,1)} %tok.1, f32[1,512]{1,0:T(1,128)} %bitcast.5, bf16[512,512]{1,0:T(8,128)(2,1)} %wq.1, bf16[512,512]{1,0:T(8,128)(2,1)} %wk.1, bf16[512,512]{1,0:T(8,128)(2,1)} %wv.1, bf16[512,512]{1,0:T(8,128)(2,1)} %wo.1, f32[1,512]{1,0:T(1,128)} %bitcast.6, ...), custom_call_target="tpu_custom_call" | custom-call | tf_op jit(solution)/shard_map/pallas_call | solution.py:597
  48.9 0.6 %copy.12 = bf16[1,104,512]{2,1,0:T(8,128)(2,1)} copy(bf16[1,104,512]{2,1,0:T(8,128)(2,1)S(1)} %shard_map.100) | data formatting | bytes 212992
